TPU v7x, 32 devices: a whole 2x2x4 slice. The times are simulated.
32 devices in a mesh: rows: 8 (over z, x), seq: 4 (over y, core).
Axes of the slice: x: 2, y: 2, z: 4, core: 2. Of those that a mesh axis runs over, the one named last changes fastest.
Arguments:
- tokens: bfloat16 [80, 512, 512], P('rows', 'seq'), may hold values from -6 to 6
- seg_ids: int32 [80, 512], P('rows', 'seq'), may hold values from 0 to 3, as said below
- w_query: bfloat16 [512, 384], replicated, may hold values from -0.25 to 0.25
- w_key: bfloat16 [512, 384], replicated, may hold values from -0.0625 to 0.0625
- w_value: bfloat16 [512, 384], replicated, may hold values from -0.25 to 0.25
- w_out: bfloat16 [384, 512], replicated, may hold values from -2.5 to 2.5
- w_gate: bfloat16 [512, 1024], replicated, may hold values from -0.25 to 0.25
- w_up: bfloat16 [512, 1024], replicated, may hold values from -0.25 to 0.25
- w_down: bfloat16 [1024, 512], replicated, may hold values from -0.1875 to 0.1875
- w_head: bfloat16 [512, 768], replicated, may hold values from -0.25 to 0.25
- norm_attn: float32 [512], replicated, may hold values from 0.5 to 1.5
- norm_ffn: float32 [512], replicated, may hold values from 0.5 to 1.5
- bucket_bias_table: float32 [32, 6], replicated, may hold values from -4 to 4
- grad_y: bfloat16 [80, 512, 512], P('rows', 'seq'), may hold values from -6 to 6
- embedding_gradient: float32 [80, 768], P('rows'), may hold values from -6 to 6
Outputs:
- block_out: bfloat16 [80, 512, 512], P('rows', 'seq')
- embedding: float32 [80, 768], P('rows')
- grad_x: bfloat16 [80, 512, 512], P('rows', 'seq')
- grad_query: float32 [512, 384], replicated
- key_weight_gradient: float32 [512, 384], replicated
- grad_value: float32 [512, 384], replicated
- grad_out: float32 [384, 512], replicated
- grad_gate: float32 [512, 1024], replicated
- grad_up: float32 [512, 1024], replicated
- grad_down: float32 [1024, 512], replicated
- grad_head: float32 [512, 768], replicated
- grad_norm_attn: float32 [512], replicated
- grad_norm_ffn: float32 [512], replicated
- grad_table: float32 [32, 6], replicated
Inputs may be any that keep to these rules, and one draw needn't show every extreme that they name: `seg_ids`: each row holds exactly three passages, numbered 1, 2, 3 in order of position, followed by padding (0) at the row's end, possibly none.
All inputs are finite; a program needn't handle non-finite values.
Results may differ from a plain program's by a relative error of at most 0.019.
Values may be sent and summed in bfloat16 or wider, within the bound.
No kernel may reach another device: no remote copies, remote signals or barrier semaphores. Data moves between devices by JAX's collectives and lax.ppermute only.
A program may use at most 192 MiB of HBM per device.

v0:
```python
import jax
import jax.numpy as jnp
from jax import lax
from jax.sharding import PartitionSpec as P

EPS = 1e-06
LIMITS = (12, 16, 23, 32, 46, 64, 91)
TOP_PRECISION = lax.Precision.HIGHEST


def bucket_index(offset):
    distance = jnp.abs(offset)
    far_bucket = 8 + sum(((distance >= threshold).astype(jnp.int32) for threshold in LIMITS))
    near_bucket = jnp.where(distance < 8, distance, far_bucket)
    return near_bucket + 16 * (offset > 0).astype(jnp.int32)


def rms_scale(values, weights):
    inverse = lax.rsqrt(jnp.mean(values * values, axis=-1, keepdims=True) + EPS)
    return values * inverse * weights


def gated_unit(gate_in, up_in):
    return jax.nn.gelu(gate_in, approximate=True) * up_in


def project(left_side, right_side):
    return jnp.dot(left_side, right_side, preferred_element_type=jnp.float32)


def project_back(left_side, right_side):
    return jnp.einsum("rto,io->rti", left_side, right_side, preferred_element_type=jnp.float32)


def weight_grad(left_side, right_side):
    return jnp.einsum("rti,rto->io", left_side, right_side, preferred_element_type=jnp.float32)


def split_heads(values, num_heads):
    return values.reshape(values.shape[0], values.shape[1], num_heads, values.shape[2] // num_heads)


def score_block(q_heads, k_heads, position_bias_block, same_seg):
    raw_scores = jnp.einsum("rqhd,rkhd->rhqk", q_heads, k_heads, preferred_element_type=jnp.float32)
    return jnp.where(same_seg[:, None], raw_scores + position_bias_block[None], -1000000000.0)


def shards(
    tokens,
    seg_ids,
    w_query,
    w_key,
    w_value,
    w_out,
    w_gate,
    w_up,
    w_down,
    w_head,
    norm_attn,
    norm_ffn,
    bucket_bias_table,
    grad_y,
    embedding_gradient,
):
    row_count, span_len, width = tokens.shape
    num_heads = bucket_bias_table.shape[1]
    seq_count = lax.axis_size("seq")
    first_pos = lax.axis_index("seq") * span_len
    all_segs = lax.all_gather(seg_ids, "seq", axis=1, tiled=True)
    row_len = all_segs.shape[1]
    same_seg = seg_ids[:, :, None] == all_segs[:, None, :]
    query_pos = first_pos + jnp.arange(span_len, dtype=jnp.int32)
    key_pos = jnp.arange(row_len, dtype=jnp.int32)
    buckets = bucket_index(key_pos[None, :] - query_pos[:, None])
    bucket_ids = jnp.arange(bucket_bias_table.shape[0], dtype=jnp.int32)
    bucket_indicator = (buckets[None] == bucket_ids[:, None, None]).astype(jnp.float32)
    position_bias_block = jnp.einsum(
        "apu,az->zpu", bucket_indicator, bucket_bias_table, precision=TOP_PRECISION
    )
    x_float = tokens.astype(jnp.float32)
    normed_one, pull_one = jax.vjp(rms_scale, x_float, norm_attn)
    normed_one = normed_one.astype(jnp.bfloat16)
    q_rows = project(normed_one, w_query).astype(jnp.bfloat16)
    k_rows = project(normed_one, w_key).astype(jnp.bfloat16)
    v_rows = project(normed_one, w_value).astype(jnp.bfloat16)
    k_all, v_all = (
        lax.all_gather(k_rows, "seq", axis=1, tiled=True),
        lax.all_gather(v_rows, "seq", axis=1, tiled=True),
    )
    q_heads = split_heads(q_rows, num_heads)
    scores = score_block(q_heads, split_heads(k_all, num_heads), position_bias_block, same_seg)
    row_max = jnp.max(scores, axis=-1, keepdims=True)
    exp_scores = jnp.exp(scores - row_max)
    row_total = jnp.sum(exp_scores, axis=-1, keepdims=True)
    log_total = row_max + jnp.log(row_total)
    prob_low = (exp_scores / row_total).astype(jnp.bfloat16)
    attended_wide = jnp.einsum(
        "rhqk,rkhd->rqhd",
        prob_low,
        split_heads(v_all, num_heads),
        preferred_element_type=jnp.float32,
    )
    attended = attended_wide.astype(jnp.bfloat16).reshape(row_count, span_len, -1)
    mid_stream = x_float + project(attended, w_out)
    normed_two, pull_two = jax.vjp(rms_scale, mid_stream, norm_ffn)
    normed_two = normed_two.astype(jnp.bfloat16)
    gate_pre = project(normed_two, w_gate)
    up_part = project(normed_two, w_up)
    hidden, pull_gate = jax.vjp(gated_unit, gate_pre, up_part)
    hidden = hidden.astype(jnp.bfloat16)
    out_float = mid_stream + project(hidden, w_down)
    valid_mask = (seg_ids != 0).astype(jnp.float32)
    counts = jnp.sum((all_segs != 0).astype(jnp.float32), axis=1)
    partial_value = jnp.sum(out_float * valid_mask[:, :, None], axis=1)
    pooled = lax.psum(partial_value, "seq") / counts[:, None]
    head_float = w_head.astype(jnp.float32)
    projected = jnp.dot(pooled, head_float, precision=TOP_PRECISION)
    inverse = lax.rsqrt(jnp.sum(projected * projected, axis=-1, keepdims=True) + EPS)
    embedding = projected * inverse
    g_proj = inverse * (
        embedding_gradient
        - embedding * jnp.sum(embedding * embedding_gradient, axis=-1, keepdims=True)
    )
    grad_head = jnp.dot(pooled.T, g_proj, precision=TOP_PRECISION) / seq_count
    g_pooled = jnp.dot(g_proj, head_float.T, precision=TOP_PRECISION) / counts[:, None]
    g_out = grad_y.astype(jnp.float32) + valid_mask[:, :, None] * g_pooled[:, None, :]
    g_branch = g_out.astype(jnp.bfloat16)
    grad_down = weight_grad(hidden, g_branch)
    g_gate, g_up = pull_gate(project_back(g_branch, w_down))
    g_gate = g_gate.astype(jnp.bfloat16)
    g_up = g_up.astype(jnp.bfloat16)
    grad_gate = weight_grad(normed_two, g_gate)
    grad_up = weight_grad(normed_two, g_up)
    g_mid_norm, grad_norm_ffn = pull_two(project_back(g_gate, w_gate) + project_back(g_up, w_up))
    g_mid = g_out + g_mid_norm
    g_attn = g_mid.astype(jnp.bfloat16)
    grad_out = weight_grad(attended, g_attn)
    g_attended = project_back(g_attn, w_out).astype(jnp.bfloat16)
    g_att_heads = split_heads(g_attended, num_heads)
    k_heads = split_heads(k_all, num_heads)
    v_heads = split_heads(v_all, num_heads)
    scores = score_block(q_heads, k_heads, position_bias_block, same_seg)
    prob_full = jnp.exp(scores - log_total)
    g_probs = jnp.einsum(
        "rqhd,rkhd->rhqk", g_att_heads, v_heads, preferred_element_type=jnp.float32
    )
    score_gradient = (
        prob_full * (g_probs - jnp.sum(g_probs * prob_full, axis=-1, keepdims=True))
    ).astype(jnp.bfloat16)
    grad_table = jnp.einsum(
        "mtx,utx->um",
        jnp.sum(score_gradient, axis=0, dtype=jnp.float32),
        bucket_indicator,
        precision=TOP_PRECISION,
    )
    g_query = jnp.einsum(
        "rhqk,rkhd->rqhd", score_gradient, k_heads, preferred_element_type=jnp.float32
    )
    g_query = g_query.astype(jnp.bfloat16).reshape(row_count, span_len, -1)
    key_terms = jnp.einsum(
        "rhqk,rqhd->rkhd", score_gradient, q_heads, preferred_element_type=jnp.float32
    ).reshape(row_count, row_len, -1)
    value_terms = jnp.einsum(
        "rhqk,rqhd->rkhd",
        prob_full.astype(jnp.bfloat16),
        g_att_heads,
        preferred_element_type=jnp.float32,
    ).reshape(row_count, row_len, -1)
    g_key, g_value = (
        lax.psum_scatter(
            key_terms.astype(jnp.bfloat16), "seq", scatter_dimension=1, tiled=True
        ).astype(jnp.float32),
        lax.psum_scatter(
            value_terms.astype(jnp.bfloat16), "seq", scatter_dimension=1, tiled=True
        ).astype(jnp.float32),
    )
    g_key = g_key.astype(jnp.bfloat16)
    g_value = g_value.astype(jnp.bfloat16)
    grad_query = weight_grad(normed_one, g_query)
    key_weight_gradient = weight_grad(normed_one, g_key)
    grad_value = weight_grad(normed_one, g_value)
    g_normed_one = (
        project_back(g_query, w_query) + project_back(g_key, w_key) + project_back(g_value, w_value)
    )
    g_x_norm, grad_norm_attn = pull_one(g_normed_one)
    grad_x = (g_mid + g_x_norm).astype(jnp.bfloat16)
    (
        grad_query,
        key_weight_gradient,
        grad_value,
        grad_out,
        grad_gate,
        grad_up,
        grad_down,
        grad_head,
        grad_norm_attn,
        grad_norm_ffn,
        grad_table,
    ) = lax.psum(
        (
            grad_query,
            key_weight_gradient,
            grad_value,
            grad_out,
            grad_gate,
            grad_up,
            grad_down,
            grad_head,
            grad_norm_attn,
            grad_norm_ffn,
            grad_table,
        ),
        ("rows", "seq"),
    )
    return (
        out_float.astype(jnp.bfloat16),
        embedding,
        grad_x,
        grad_query,
        key_weight_gradient,
        grad_value,
        grad_out,
        grad_gate,
        grad_up,
        grad_down,
        grad_head,
        grad_norm_attn,
        grad_norm_ffn,
        grad_table,
    )


def solution(mesh):
    return jax.shard_map(
        shards,
        mesh=mesh,
        in_specs=(
            P("rows", "seq", None),
            P("rows", "seq"),
            P(),
            P(),
            P(),
            P(),
            P(),
            P(),
            P(),
            P(),
            P(),
            P(),
            P(),
            P("rows", "seq", None),
            P("rows", None),
        ),
        out_specs=(
            P("rows", "seq", None),
            P("rows", None),
            P("rows", "seq", None),
            P(),
            P(),
            P(),
            P(),
            P(),
            P(),
            P(),
            P(),
            P(),
            P(),
            P(),
        ),
        check_vma=False,
    )
```

profile of v0, /device:TPU:0, one launch (start us, length us, event | category | flops | bytes accessed | tf_op | source)
XLA Modules:
  0.0 503.5 jit_solution(15133024722548707181)
XLA Ops:
  7.2 1.7 fusion.24
  9.6 3.4 convolution_convert_fusion.2
  13.1 1.8 convolution_convert_fusion.4
  15.0 1.8 convolution_convert_fusion.3
  16.9 1.6 copy.66
  18.8 2.7 fusion.31
  21.5 2.1 copy.68
  23.6 6.4 %all_gather.10 = s32[10,512]{1,0:T(8,128)S(1)} all-gather(s32[10,128]{1,0:T(8,128)S(1)} %copy-done.43), channel_id=1, replica_groups=mesh['rows'=8,'seq'=4] {'seq'}, dimensions={1}, use_global_device_ids=true | all-gather | bytes 25600 | tf_op jit(solution)/shard_map/all_gather | solution.py:69
  31.4 17.6 %all-gather.5.cloned.1.call-done = bf16[10,512,384]{2,1,0:T(8,128)(2,1)} async-done(((bf16[10,128,384]{2,1,0:T(8,128)(2,1)}), bf16[10,512,384]{2,1,0:T(8,128)(2,1)}) %all-gather.5.cloned.1.call-update) | async-done | bytes 3932176 | tf_op jit(solution)/shard_map/all_gather | solution.py:87
  49.0 6.3 %copy.67 = bf16[10,512,384]{1,2,0:T(8,128)(2,1)} copy(bf16[10,512,384]{2,1,0:T(8,128)(2,1)} %all-gather.5.cloned.1.call-done) | data formatting | bytes 7864320 | tf_op jit(solution)/shard_map/all_gather | solution.py:87
  55.3 7.1 %fusion.80 = (f32[10,6,128]{2,1,0:T(8,128)S(1)}, f32[10,6,128,512]{3,2,1,0:T(8,128)S(1)}) fusion(f32[6,128,512]{2,1,0:T(8,128)} %copy.68, bf16[10,128,6,64]{1,3,2,0:T(8,128)(2,1)S(1)} %bitcast.120, bf16[10,512,6,64]{1,3,2,0:T(8,128)(2,1)} %bitcast.114, pred[10,128,512]{2,1,0:T(8,128)(4,1)} %broadcast_compare_fusion), kind=kOutput, calls=%fused_computation.128 | convolution fusion | flops 515105280 | bytes 22902784 | tf_op jit(solution)/shard_map/rqhd,rkhd->rhqk/dot_general | solution.py:44
  62.4 3.8 fusion
  66.2 1.6 copy-done.2
  67.9 16.3 %all-gather.3.cloned.1.call-done = bf16[10,512,384]{2,1,0:T(8,128)(2,1)} async-done(((bf16[10,128,384]{2,1,0:T(8,128)(2,1)}), bf16[10,512,384]{2,1,0:T(8,128)(2,1)}) %all-gather.3.cloned.1.call-update) | async-done | bytes 3932176 | tf_op jit(solution)/shard_map/all_gather | solution.py:88
  84.2 6.2 %copy.65 = bf16[10,512,384]{1,2,0:T(8,128)(2,1)} copy(bf16[10,512,384]{2,1,0:T(8,128)(2,1)} %all-gather.3.cloned.1.call-done) | data formatting | bytes 7864320 | tf_op jit(solution)/shard_map/all_gather | solution.py:88
  90.4 8.8 %fusion.32 = bf16[10,6,64,128]{3,2,1,0:T(8,128)(2,1)S(1)} fusion(bf16[10,512,6,64]{1,3,2,0:T(8,128)(2,1)} %bitcast.118, f32[10,6,128,512]{3,2,1,0:T(8,128)} %copy-done.2, f32[10,6,128]{2,1,0:T(8,128)S(1)} %fusion, f32[10,6,128]{2,1,0:T(8,128)S(1)} %get-tuple-element.37), kind=kOutput, calls=%fused_computation.63 | convolution fusion | flops 515604480 | bytes 20705280 | tf_op jit(solution)/shard_map/rhqk,rkhd->rqhd/dot_general | solution.py:97
  100.6 1.7 copy-done.28
  104.0 4.2 multiply_convert_fusion.2
  108.2 2.7 multiply_reduce_fusion.3
  110.9 10.9 %psum.84 = f32[10,512]{1,0:T(8,128)S(1)} all-reduce(f32[10,512]{1,0:T(8,128)S(1)} %get-tuple-element.35), channel_id=1, replica_groups=mesh['rows'=8,'seq'=4] {'seq'}, use_global_device_ids=true, to_apply=%region_5.6 | all-reduce | flops 5120 | bytes 40960 | tf_op jit(solution)/shard_map/psum | solution.py:115
  121.8 1.7 multiply_reduce_fusion.6
  123.7 1.9 convolution_divide_fusion
  125.6 8.4 %multiply_convert_fusion.1 = (bf16[10,128,1024]{2,1,0:T(8,128)(2,1)S(1)}, bf16[10,128,1024]{2,1,0:T(8,128)(2,1)S(1)}) fusion(f32[10,128,1024]{2,1,0:T(8,128)} %copy-done.13, f32[10,128,1024]{2,1,0:T(8,128)} %get-tuple-element.42, bf16[1024,512]{1,0:T(8,128)(2,1)S(1)} %copy-done, bf16[10,128,512]{2,1,0:T(8,128)(2,1)} %param.28, ...), kind=kOutput, calls=%fused_computation.24 | convolution fusion | flops 1376256000 | bytes 18113536 | tf_op jit(solution)/shard_map/rto,io->rti/dot_general | solution.py:32
  137.9 2.8 multiply_reduce_fusion.1
  143.3 1.8 convolution_convert_fusion.1
  145.2 1.6 copy.70
  146.8 8.3 %fusion.27 = bf16[10,6,64,512]{3,2,1,0:T(8,128)(2,1)} fusion(bf16[10,128,6,64]{1,3,2,0:T(8,128)(2,1)S(1)} %bitcast.122, f32[10,6,128,512]{3,2,1,0:T(8,128)} %copy-done.2, f32[10,6,128]{2,1,0:T(8,128)S(1)} %log_add_fusion), kind=kOutput, calls=%fused_computation.53 | convolution fusion | flops 513146880 | bytes 20674560 | tf_op jit(solution)/shard_map/rhqk,rqhd->rkhd/dot_general | solution.py:163
  155.1 6.2 %copy.73 = bf16[10,512,384]{2,1,0:T(8,128)(2,1)} copy(bf16[10,512,384]{1,2,0:T(8,128)(2,1)} %bitcast.117) | data formatting | bytes 7864320 | tf_op jit(solution)/shard_map/convert_element_type | solution.py:174
  161.4 12.7 %multiply_reduce_fusion = (f32[10,6,128]{2,1,0:T(8,128)S(1)}, f32[10,6,128,512]{3,2,1,0:T(8,128)}) fusion(f32[10,6,128,512]{3,2,1,0:T(8,128)} %copy-done.2, f32[10,6,128]{2,1,0:T(8,128)S(1)} %log_add_fusion, bf16[10,128,6,64]{1,3,2,0:T(8,128)(2,1)S(1)} %bitcast.123, bf16[10,512,6,64]{1,3,2,0:T(8,128)(2,1)} %bitcast.119), kind=kOutput, calls=%fused_computation.2 | convolution fusion | flops 515105280 | bytes 36433920 | tf_op jit(solution)/shard_map/rqhd,rkhd->rhqk/dot_general | solution.py:144
  174.1 13.0 %convert_reduce_fusion = (f32[6,128,512]{2,1,0:T(8,128)}, bf16[10,6,128,512]{3,2,1,0:T(8,128)(2,1)S(1)}) fusion(f32[10,6,128,512]{3,2,1,0:T(8,128)} %get-tuple-element.48, f32[10,6,128]{2,1,0:T(8,128)S(1)} %get-tuple-element.47, f32[10,6,128,512]{3,2,1,0:T(8,128)} %copy-done.2, f32[10,6,128]{2,1,0:T(8,128)S(1)} %log_add_fusion), kind=kLoop, calls=%fused_computation | loop fusion | flops 23199744 | bytes 40955904 | tf_op jit(solution)/shard_map/reduce_sum | solution.py:152
  187.0 3.6 convolution_convert_fusion
  191.3 6.2 %copy.72 = bf16[10,512,384]{2,1,0:T(8,128)(2,1)} copy(bf16[10,512,384]{1,2,0:T(8,128)(2,1)} %bitcast.116) | data formatting | bytes 7864320 | tf_op jit(solution)/shard_map/convert_element_type | solution.py:171
  198.2 2.7 convolution_multiply_fusion
  200.9 7.2 %convolution_convert_fusion.5 = bf16[10,6,64,128]{3,2,1,0:T(8,128)(2,1)S(1)} fusion(bf16[10,512,6,64]{1,3,2,0:T(8,128)(2,1)} %bitcast.115, bf16[10,6,128,512]{3,2,1,0:T(8,128)(2,1)} %copy-done.3), kind=kOutput, calls=%fused_computation.68 | convolution fusion | flops 503808000 | bytes 12779520 | tf_op jit(solution)/shard_map/rhqk,rkhd->rqhd/dot_general | solution.py:156
  208.2 2.1 convolution_bitcast_fusion.6
  212.7 2.9 convolution_bitcast_fusion.1
  215.5 2.9 convolution_bitcast_fusion.2
  219.2 3.0 convolution_bitcast_fusion
  222.1 3.1 convolution_bitcast_fusion.4
  225.2 25.7 %reduce-scatter.3.cloned.1.call-done = bf16[10,128,384]{2,1,0:T(8,128)(2,1)} async-done(((bf16[10,512,384]{2,1,0:T(8,128)(2,1)}), bf16[10,128,384]{2,1,0:T(8,128)(2,1)}) %reduce-scatter.3.cloned.1.call-update) | async-done | bytes 983056 | tf_op jit(solution)/shard_map/reduce_scatter | solution.py:170
  250.9 3.1 convolution_bitcast_fusion.5
  255.0 6.0 %fusion.33 = f32[32,6]{0,1:T(8,128)S(1)} fusion(f32[6,128,512]{2,1,0:T(8,128)} %get-tuple-element.29, s32[128,512]{1,0:T(8,128)S(1)} %copy-done.27), kind=kOutput, calls=%fused_computation.75 | convolution fusion | flops 153092096 | bytes 1835776 | tf_op jit(solution)/shard_map/mtx,utx->um/dot_general | solution.py:150
  263.5 3.0 fusion.20
  266.6 40.4 %all-reduce = (f32[512]{0:T(512)}, f32[512]{0:T(512)}, f32[32,6]{0,1:T(8,128)}) all-reduce(f32[512]{0:T(512)S(1)} %get-tuple-element.16, f32[512]{0:T(512)S(1)} %copy-done.59, f32[32,6]{0,1:T(8,128)S(1)} %fusion.33), channel_id=1, replica_groups=mesh['rows'=8,'seq'=4] {'rows','seq'}, use_global_device_ids=true, to_apply=%region_23.24 | all-reduce | flops 1216 | bytes 9728 | tf_op jit(solution)/shard_map/psum | solution.py:199
  307.0 4.5 fusion.23
  311.4 172.2 %all-reduce.4.cloned.1.call-done = (f32[512,384]{1,0:T(8,128)}, f32[512,384]{1,0:T(8,128)}, f32[512,384]{1,0:T(8,128)}, f32[384,512]{1,0:T(8,128)}, f32[512,1024...) async-done(((f32[512,384]{1,0:T(8,128)}, f32[512,384]{1,0:T(8,128)}, f32[512,384]{1,0:T(8,128)}, f32[384,512]{1,0:T(8,128)}, ...) | async-done | bytes 11010064 | tf_op jit(solution)/shard_map/psum | solution.py:199
  483.6 2.2 copy.103
  485.8 2.2 copy.104
  (169 shorter events, 29.0 us)
Async XLA Ops:
  7.2 101.0 %copy-start = (bf16[1024,512]{1,0:T(8,128)(2,1)S(1)}, bf16[1024,512]{1,0:T(8,128)(2,1)}, u32[]{:S(2)}) copy-start(bf16[1024,512]{1,0:T(8,128)(2,1)} %param.23) | copy-start | bytes 3145732
  7.2 41.8 %all-gather.5.cloned.1.call-start = ((), (), s32[]{:S(2)}) async-start(), calls=%async_computation.3 | async-start | bytes 4915200 | tf_op jit(solution)/shard_map/all_gather | solution.py:87
  9.6 3.5 copy-start.8
  9.6 3.5 copy-start.38
  9.6 3.5 copy-start.55
  9.6 5.4 %copy-start.48 = (f32[10,128]{1,0:T(8,128)}, f32[10,128]{1,0:T(8,128)S(1)}, u32[]{:S(2)}) copy-start(f32[10,128]{1,0:T(8,128)S(1)} %fusion.70) | copy-start | bytes 15364
  13.0 71.2 %all-gather.3.cloned.1.call-start = ((), (), s32[]{:S(2)}) async-start(), calls=%async_computation.2 | async-start | bytes 4915200 | tf_op jit(solution)/shard_map/all_gather | solution.py:88
  14.9 207.2 %reduce-scatter.5.cloned.1.call-start = ((), (), s32[]{:S(2)}) async-start(), calls=%async_computation.5 | async-start | bytes 4915200 | tf_op jit(solution)/shard_map/reduce_scatter | solution.py:173
  15.0 3.8 copy-start.64
  18.8 4.7 copy-start.26
  18.8 4.7 copy-start.43
  30.1 91.7 %copy-start.57 = (f32[10]{0:T(128)}, f32[10]{0:T(128)S(1)}, u32[]{:S(2)}) copy-start(f32[10]{0:T(128)S(1)} %convert_reduce_fusion.1) | copy-start | bytes 124
  30.1 78.1 %copy-start.50 = (f32[10,128]{1,0:T(8,128)}, f32[10,128]{1,0:T(8,128)S(1)}, u32[]{:S(2)}) copy-start(f32[10,128]{1,0:T(8,128)S(1)} %compare_convert_fusion) | copy-start | bytes 15364
  62.4 5.4 %copy-start.2 = (f32[10,6,128,512]{3,2,1,0:T(8,128)}, f32[10,6,128,512]{3,2,1,0:T(8,128)S(1)}, u32[]{:S(2)}) copy-start(f32[10,6,128,512]{3,2,1,0:T(8,128)S(1)} %get-tuple-element.38) | copy-start | bytes 47185924
  90.4 8.8 %copy-start.22 = (bf16[384,512]{1,0:T(8,128)(2,1)S(1)}, bf16[384,512]{1,0:T(8,128)(2,1)}, u32[]{:S(2)}) copy-start(bf16[384,512]{1,0:T(8,128)(2,1)} %param.20) | copy-start | bytes 1179652
  100.2 3.6 copy-start.46
  100.3 7.9 %copy-start.6 = (f32[10,128,512]{2,1,0:T(8,128)}, f32[10,128,512]{2,1,0:T(8,128)S(1)}, u32[]{:S(2)}) copy-start(f32[10,128,512]{2,1,0:T(8,128)S(1)} %get-tuple-element.40) | copy-start | bytes 7864324
  104.0 4.2 copy-start.13
  108.2 2.7 copy-start.65
  108.2 15.3 %copy-start.36 = (f32[10,768]{1,0:T(8,128)S(1)}, f32[10,768]{1,0:T(8,128)}, u32[]{:S(2)}) copy-start(f32[10,768]{1,0:T(8,128)} %param.29) | copy-start | bytes 92164
  123.7 74.1 %copy-start.37 = (f32[10,768]{1,0:T(8,128)}, f32[10,768]{1,0:T(8,128)S(1)}, u32[]{:S(2)}) copy-start(f32[10,768]{1,0:T(8,128)S(1)} %get-tuple-element.51) | copy-start | bytes 92164
  125.6 8.4 %copy-start.29 = (bf16[512,1024]{1,0:T(8,128)(2,1)S(1)}, bf16[512,1024]{1,0:T(8,128)(2,1)}, u32[]{:S(2)}) copy-start(bf16[512,1024]{1,0:T(8,128)(2,1)} %param.21) | copy-start | bytes 3145732
  134.0 2.7 copy-start.11
  134.0 3.6 copy-start.7
  134.1 3.9 copy-start.31
  134.1 3.9 copy-start.54
  137.9 2.8 copy-start.47
  137.9 2.8 copy-start.24
  137.9 2.8 copy-start.51
  140.8 2.5 copy-start.23
  161.3 89.6 %reduce-scatter.3.cloned.1.call-start = ((), (), s32[]{:S(2)}) async-start(), calls=%async_computation.4 | async-start | bytes 4915200 | tf_op jit(solution)/shard_map/reduce_scatter | solution.py:170
  187.0 4.3 copy-start.3
  197.6 286.0 %all-reduce.4.cloned.1.call-start = ((), (), s32[]{:S(2)}) async-start(), calls=%async_computation.6 | async-start | bytes 22020096 | tf_op jit(solution)/shard_map/psum | solution.py:199
  200.9 7.3 %copy-start.49 = (f32[10,128]{1,0:T(8,128)S(1)}, f32[10,128]{1,0:T(8,128)}, u32[]{:S(2)}) copy-start(f32[10,128]{1,0:T(8,128)} %copy-done.48) | copy-start | bytes 15364
  200.9 7.3 %copy-start.56 = (f32[512]{0:T(512)S(1)}, f32[512]{0:T(512)}, u32[]{:S(2)}) copy-start(f32[512]{0:T(512)} %param.25) | copy-start | bytes 6148
  210.2 2.4 copy-start.12
  212.7 2.9 copy-start.17
  215.5 2.9 copy-start.25
  215.5 2.9 copy-start.52
  215.5 3.6 copy-start.66
  254.0 6.9 %copy-start.41 = (bf16[512,384]{1,0:T(8,128)(2,1)S(1)}, bf16[512,384]{1,0:T(8,128)(2,1)}, u32[]{:S(2)}) copy-start(bf16[512,384]{1,0:T(8,128)(2,1)} %param.17) | copy-start | bytes 1179652
  263.5 3.0 copy-start.59
  263.5 43.4 %copy-start.45 = (f32[10,128]{1,0:T(8,128)S(1)}, f32[10,128]{1,0:T(8,128)}, u32[]{:S(2)}) copy-start(f32[10,128]{1,0:T(8,128)} %copy-done.44) | copy-start | bytes 15364
  483.6 4.4 copy-start.35
  483.6 5.3 %copy-start.34 = (f32[384,512]{1,0:T(8,128)S(1)}, f32[384,512]{1,0:T(8,128)}, u32[]{:S(2)}) copy-start(f32[384,512]{1,0:T(8,128)} %get-tuple-element.56) | copy-start | bytes 2359300
  485.8 4.0 copy-start.20
  491.1 2.3 copy-start.18
  493.5 3.3 copy-start.1
  (24 other events, 35.3 us)
Sparse Core Ops, SparseCore 0:
  13.1 35.8 all-gather.4
  51.1 32.9 all-gather.2
  161.4 43.9 reduce-scatter.4
  208.0 42.8 reduce-scatter.2
  258.4 225.2 all-reduce.3
where the time goes:
time: 510 us; the launch traced here: 504 us
  waiting for transfers between devices  232 us (45%)
  matrix products  117 us (23%)
  blocking collectives  57.6 us (11%)
  local copies, waits for them, and re-layouts  55.8 us (11%)
  other arithmetic  26.3 us (5%)
  between operations  14.7 us (3%)
    psum x1, waiting for transfers between devices, shards(): lax.psum((grad_query, key_weight_gradient, grad_value, grad_out, grad_gat...  172 us
    psum x1, blocking collectives, shards(): lax.psum((grad_query, key_weight_gradient, grad_value, grad_out, grad_gat...  40.4 us
    reduce_scatter x1, waiting for transfers between devices, shards(): lax.psum_scatter(key_terms.astype(jnp.bfloat16), 'seq', scatter_dimension...  25.7 us
    unnamed x142, local copies, waits for them, and re-layouts  25.5 us
    dot_general x7, matrix products, project_back(): jnp.einsum('rto,io->rti', left_side, right_side, preferred_element_type=j...  19.3 us
    dot_general x7, matrix products, weight_grad(): jnp.einsum('rti,rto->io', left_side, right_side, preferred_element_type=j...  18.5 us
    all_gather x1, waiting for transfers between devices, shards(): lax.all_gather(k_rows, 'seq', axis=1, tiled=True)  17.6 us
    dot_general x7, matrix products, project(): return jnp.dot(left_side, right_side, preferred_element_type=jnp.float32)  16.4 us
  transfers between devices with their start and end apart: 5, of which 4 were waited for; matrix products, arithmetic and copies ran while one was open for 21% of the time, Pallas kernels for 0%

commit v1 on v0

v1 whole, which is shorter than its diff:
```python
import functools

import jax
import jax.numpy as jnp
from jax import lax
from jax.experimental import pallas as pl
from jax.experimental.pallas import tpu as pltpu
from jax.sharding import PartitionSpec as P

EPS = 1e-06
LIMITS = (12, 16, 23, 32, 46, 64, 91)
TOP_PRECISION = lax.Precision.HIGHEST
F32 = jnp.float32
BF16 = jnp.bfloat16
MASK_STEP = 2.0**30
VMEM = pl.BlockSpec(memory_space=pltpu.VMEM)
SMEM = pl.BlockSpec(memory_space=pltpu.SMEM)
PARAMS = pltpu.CompilerParams(vmem_limit_bytes=56 * 2**20)
LANES = 128


def mm(a, b):
    return lax.dot_general(a, b, (((1,), (0,)), ((), ())), preferred_element_type=F32)


def mm_nt(a, b):
    return lax.dot_general(a, b, (((1,), (1,)), ((), ())), preferred_element_type=F32)


def bucket_index(offset):
    distance = jnp.abs(offset)
    far_bucket = 8 + sum(((distance >= threshold).astype(jnp.int32) for threshold in LIMITS))
    near_bucket = jnp.where(distance < 8, distance, far_bucket)
    return near_bucket + 16 * (offset > 0).astype(jnp.int32)


def parts3(v):
    hi = v.astype(BF16).astype(F32)
    mid = (v - hi).astype(BF16).astype(F32)
    low = (v - hi - mid).astype(BF16).astype(F32)
    row = lax.broadcasted_iota(jnp.int32, v.shape, 0)
    return jnp.where(row == 0, hi, jnp.where(row == 1, mid, jnp.where(row == 2, low, 0.0))).astype(BF16)


def wide_dot(row, mat, dot):
    out = dot(parts3(jnp.broadcast_to(row, (16, row.shape[1]))), mat)
    return jnp.sum(out, axis=0, keepdims=True)


def diagonal_sums(table):
    height, width = table.shape
    acc = table[0:8, :]
    for u in range(8, height, 8):
        acc += pltpu.roll(table[u : u + 8, :], width - u, 1)
    row = lax.broadcasted_iota(jnp.int32, acc.shape, 0)
    for bit in (1, 2, 4):
        acc = jnp.where((row & bit) != 0, pltpu.roll(acc, width - bit, 1), acc)
    return jnp.sum(acc, axis=0, keepdims=True)


def bias_kernel(g_ref, t_ref):
    heads, _, width = t_ref.shape
    for h in range(heads):
        line = jnp.broadcast_to(g_ref[h : h + 1, :], (LANES, width))
        t_ref[h] = pltpu.roll(line, 0, 1, stride=1, stride_axis=0)


def forward_kernel(
    slot, n,
    meta, x0, x1, x2, x3, bias, wqkv_t, wout_t, wg_t, wu_t, wd_t, nattn, nffn,
    q_o, v_o, kt_o, p_o, att_o, x_o, mid_o, a_o, ge_o, hid_o, pooled_o, b0, b1, b2, b3,
    seg, n1, kk, tok,
):
    width = wqkv_t.shape[1]
    inner = wout_t.shape[1]
    heads = bias.shape[0]
    head = inner // heads
    span = x0.shape[0] - 16
    length = n * span

    @pl.when(meta[1 + slot] == 1)
    def _():
        me = meta[0]
        for k, piece in enumerate((x0, x1, x2, x3)):
            at = pl.multiple_of((me ^ k) * span, span)
            tok[pl.ds(at, span), :] = piece[:span, :].astype(F32)
            seg[:, pl.ds(at, span)] = jnp.broadcast_to(piece[span : span + 1, :span].astype(F32), (LANES, span))
        for c in range(n):
            blk = tok[c * span : (c + 1) * span, :].T
            x_o[:, c * span : (c + 1) * span] = blk.astype(BF16)
            inv = lax.rsqrt(jnp.mean(blk * blk, axis=0, keepdims=True) + EPS)
            n1[:, c * span : (c + 1) * span] = (blk * inv * nattn[...]).astype(BF16)
        ids = lax.broadcasted_iota(jnp.int32, (LANES, length), 0).astype(F32)
        one = (seg[...] == ids).astype(F32)
        q_aug = one.astype(BF16)
        k_aug = ((one - 1.0) * MASK_STEP).T.astype(BF16)
        qt = mm(wqkv_t[:inner, :], n1[...]).astype(BF16)
        kt = mm(wqkv_t[inner : 2 * inner, :], n1[...])
        vt = mm(wqkv_t[2 * inner :, :], n1[...])
        kt_o[...] = kt.astype(BF16)
        q_o[...] = qt.astype(F32).T.astype(BF16)
        v_o[...] = vt.T.astype(BF16)
        k_nat = kt.T.astype(BF16)
        vt = vt.astype(BF16)
        for pair in range(heads // 2):
            kk[pair, :, :LANES] = k_nat[:, pair * LANES : (pair + 1) * LANES]
            kk[pair, :, LANES:] = k_aug
        half = length // 2
        zeros = jnp.zeros((head, half), BF16)
        for h in range(heads):
            for qc in range(2):
                qs = slice(qc * half, (qc + 1) * half)
                q_h = qt[h * head : (h + 1) * head, qs]
                rhs = jnp.concatenate([q_h, zeros, q_aug[:, qs]] if h % 2 == 0 else [zeros, q_h, q_aug[:, qs]], axis=0)
                s = []
                top = None
                for a in range(n):
                    start = (n - 1 - a) * LANES + qc * half
                    s_a = mm(kk[h // 2, a * LANES : (a + 1) * LANES, :], rhs) + bias[h, :, start : start + half]
                    s.append(s_a)
                    m_a = jnp.max(s_a, axis=0, keepdims=True)
                    top = m_a if top is None else jnp.maximum(top, m_a)
                e = [jnp.exp(s_a - top) for s_a in s]
                total = sum(jnp.sum(e_a, axis=0, keepdims=True) for e_a in e)
                scale = 1.0 / total
                for a in range(n):
                    p_o[h, a * LANES : (a + 1) * LANES, qs] = (e[a] * scale).astype(BF16)
                att_o[h * head : (h + 1) * head, qs] = mm(
                    vt[h * head : (h + 1) * head, :], p_o[h, :, qs]
                ).astype(BF16)
        mid_o[...] = x_o[...].astype(F32) + mm(wout_t[...], att_o[...])
        for c in range(n):
            blk = mid_o[:, c * span : (c + 1) * span]
            inv = lax.rsqrt(jnp.mean(blk * blk, axis=0, keepdims=True) + EPS)
            n1[:, c * span : (c + 1) * span] = (blk * inv * nffn[...]).astype(BF16)
        ff = wg_t.shape[0]
        step = 256
        for c in range(ff // step):
            cs = slice(c * step, (c + 1) * step)
            gate = mm(wg_t[cs, :], n1[...])
            up = mm(wu_t[cs, :], n1[...])
            sq = gate * gate
            th = jnp.tanh(0.7978845608028654 * gate * (1.0 + 0.044715 * sq))
            half_th = 0.5 * (1.0 + th)
            gelu = gate * half_th
            slope = half_th + (0.5 * 0.7978845608028654) * gate * (1.0 - th * th) * (1.0 + (3 * 0.044715) * sq)
            hid_o[cs, :] = (gelu * up).astype(BF16)
            a_o[cs, :] = (up * slope).astype(BF16)
            ge_o[cs, :] = gelu.astype(BF16)
        tok[...] = mid_o[...] + mm(wd_t[...], hid_o[...])
        valid = (seg[0:1, :] != 0.0).astype(F32)
        count = jnp.sum(valid, axis=1, keepdims=True)
        part = None
        for c in range(n):
            blk = tok[:, c * span : (c + 1) * span] * valid[:, c * span : (c + 1) * span]
            part = blk if part is None else part + blk
        pooled = jnp.sum(part.T, axis=0, keepdims=True) / count
        pooled_o[...] = jnp.broadcast_to(pooled, pooled_o.shape)
        for k, out in enumerate((b0, b1, b2, b3)):
            at = pl.multiple_of((me ^ k) * span, span)
            out[...] = tok[:, pl.ds(at, span)].T.astype(BF16)


def middle_kernel(
    slot, n,
    meta, g0, g1, g2, g3, x0, x1, x2, x3, eg, pooled, mid, a_in, ge_in, w_head, w_down, w_gate, w_up, w_out, nffn,
    n2_o, gb_o, gg_o, gu_o, ga_o, gatt_o, gnf_o, emb_o, pg_o,
    tok, seg,
):
    span = g0.shape[0]
    width = g0.shape[1]

    @pl.when(meta[1 + slot] == 1)
    def _():
        me = meta[0]
        for k, (piece, xp) in enumerate(zip((g0, g1, g2, g3), (x0, x1, x2, x3))):
            at = pl.multiple_of((me ^ k) * span, span)
            tok[pl.ds(at, span), :] = piece[...].astype(F32)
            seg[:, pl.ds(at, span)] = jnp.broadcast_to(xp[span : span + 1, :span].astype(F32), (8, span))
        valid = (seg[0:1, :] != 0.0).astype(F32)
        count = jnp.sum(valid, axis=1, keepdims=True)
        pool = pooled[0:1, :]
        proj = wide_dot(pool, w_head[...], mm)
        inv = lax.rsqrt(jnp.sum(proj * proj, axis=1, keepdims=True) + EPS)
        emb = proj * inv
        cot = eg[pl.ds(meta[4] + slot, 1), :]
        g_proj = inv * (cot - emb * jnp.sum(emb * cot, axis=1, keepdims=True))
        emb_o[...] = jnp.broadcast_to(emb, emb_o.shape)
        pg_o[:, :width] = jnp.broadcast_to(pool, (8, width))
        pg_o[:, width:] = jnp.broadcast_to(g_proj, (8, g_proj.shape[1]))
        g_pool = wide_dot(g_proj, w_head[...], mm_nt) / count
        g_col = jnp.broadcast_to(g_pool, (span, width)).T
        gout = []
        for c in range(n):
            cs = slice(c * span, (c + 1) * span)
            blk = tok[cs, :].T + valid[:, cs] * g_col
            gout.append(blk)
            gb_o[:, cs] = blk.astype(BF16)
        ff = w_down.shape[0]
        step = 256
        for c in range(ff // step):
            cs = slice(c * step, (c + 1) * step)
            g_hid = mm(w_down[cs, :], gb_o[...])
            gg_o[cs, :] = (g_hid * a_in[cs, :].astype(F32)).astype(BF16)
            gu_o[cs, :] = (g_hid * ge_in[cs, :].astype(F32)).astype(BF16)
        tok[...] = mm(w_gate[...], gg_o[...]) + mm(w_up[...], gu_o[...])
        part = None
        for c in range(n):
            cs = slice(c * span, (c + 1) * span)
            m = mid[:, cs]
            inv2 = lax.rsqrt(jnp.mean(m * m, axis=0, keepdims=True) + EPS)
            hat = m * inv2
            n2_o[:, cs] = (hat * nffn[...]).astype(BF16)
            gn = tok[:, cs]
            c2 = gn * nffn[...]
            part = gn * hat if part is None else part + gn * hat
            mean = jnp.mean(c2 * hat, axis=0, keepdims=True)
            ga_o[:, cs] = (gout[c] + inv2 * (c2 - hat * mean)).astype(BF16)
        gnf_o[...] = jnp.broadcast_to(jnp.sum(part.T, axis=0, keepdims=True), gnf_o.shape)
        gatt_o[...] = mm(w_out[...], ga_o[...]).astype(BF16)


def early_grads_kernel(last, meta, *refs):
    slots = [refs[i * 7 : (i + 1) * 7] for i in range(3)]
    out, acc = refs[21], refs[22]
    ff = slots[0][0].shape[0]
    width = slots[0][1].shape[0]
    inner = slots[0][5].shape[0]
    pieces = []
    for c in range(2):
        pieces.append((c * 512, 512, lambda s, c=c: (s[2][...], s[3][c * 512 : (c + 1) * 512, :])))
    for c in range(2):
        pieces.append((ff + c * 512, 512, lambda s, c=c: (s[2][...], s[4][c * 512 : (c + 1) * 512, :])))
    for c in range(2):
        pieces.append((2 * ff + c * width, width, lambda s, c=c: (s[0][c * width : (c + 1) * width, :], s[1][...])))
    pieces.append((2 * ff + 2 * width, inner, lambda s: (s[6][...], s[5][...])))
    for at, size, get in pieces:
        acc[:, at : at + size] = mm_nt(*get(slots[0])) + mm_nt(*get(slots[1]))

    @pl.when(meta[1 + last] == 1)
    def _():
        for at, size, get in pieces:
            acc[:, at : at + size] += mm_nt(*get(slots[2]))

    out[...] = acc[...].astype(BF16)


def backward_kernel(
    slot, n,
    meta, q_nat, v_nat, kt, p_in, att, xt, gatt, ga, w_qkv, nattn,
    n1_o, gqkv_o, line_o, gna_o, o0, o1, o2, o3,
    gs, table, tok,
):
    heads = p_in.shape[0]
    inner = kt.shape[0]
    head = inner // heads
    length = kt.shape[1]
    span = length // n
    lane = lax.broadcasted_iota(jnp.int32, (length, LANES), 1)

    @pl.when(meta[1 + slot] == 1)
    def _():
        me = meta[0]
        gatt_nat = gatt[...].astype(F32).T.astype(BF16)
        zeros = jnp.zeros((head, length), BF16)
        for pair in range(heads // 2):
            ps = slice(pair * LANES, (pair + 1) * LANES)
            gk = []
            gv = []
            for side in range(2):
                h = pair * 2 + side
                hs = slice(h * head, (h + 1) * head)
                g_h = gatt[hs, :]
                delta = jnp.sum(g_h.astype(F32) * att[hs, :].astype(F32), axis=0, keepdims=True)
                rhs = jnp.concatenate([g_h, zeros] if side == 0 else [zeros, g_h], axis=0)
                table[...] = jnp.zeros_like(table)
                for a in range(n):
                    ks = slice(a * LANES, (a + 1) * LANES)
                    g_p = mm(v_nat[ks, ps], rhs)
                    g_s = (p_in[h, ks, :].astype(F32) * (g_p - delta)).astype(BF16)
                    gs[ks, :] = g_s
                    start = (n - 1 - a) * LANES
                    table[:, start : start + length] += g_s.astype(F32)
                line_o[h : h + 1, :] = diagonal_sums(table)
                gqkv_o[hs, :] = mm(kt[hs, :], gs[...]).astype(BF16)
                gk.append(mm(gs[...], q_nat[:, ps]))
                gv.append(mm(p_in[h], gatt_nat[:, ps]))
            gk = jnp.where(lane < head, gk[0], gk[1])
            gv = jnp.where(lane < head, gv[0], gv[1])
            gqkv_o[inner + pair * LANES : inner + (pair + 1) * LANES, :] = gk.T.astype(BF16)
            gqkv_o[2 * inner + pair * LANES : 2 * inner + (pair + 1) * LANES, :] = gv.T.astype(BF16)
        tok[...] = mm(w_qkv[...], gqkv_o[...])
        part = None
        for c in range(n):
            cs = slice(c * span, (c + 1) * span)
            x = xt[:, cs].astype(F32)
            inv = lax.rsqrt(jnp.mean(x * x, axis=0, keepdims=True) + EPS)
            hat = x * inv
            n1_o[:, cs] = (hat * nattn[...]).astype(BF16)
            gn = tok[:, cs]
            c1 = gn * nattn[...]
            part = gn * hat if part is None else part + gn * hat
            mean = jnp.mean(c1 * hat, axis=0, keepdims=True)
            tok[:, cs] = ga[:, cs].astype(F32) + inv * (c1 - hat * mean)
        gna_o[...] = jnp.broadcast_to(jnp.sum(part.T, axis=0, keepdims=True), gna_o.shape)
        for k, out in enumerate((o0, o1, o2, o3)):
            at = pl.multiple_of((me ^ k) * span, span)
            out[...] = tok[:, pl.ds(at, span)].T.astype(BF16)


def late_grads_kernel(last, meta, n1_0, g_0, n1_1, g_1, n1_2, g_2, out, acc):
    acc[...] = mm_nt(n1_0[...], g_0[...]) + mm_nt(n1_1[...], g_1[...])

    @pl.when(meta[1 + last] == 1)
    def _():
        acc[...] += mm_nt(n1_2[...], g_2[...])

    out[...] = acc[...].astype(BF16)


def call(kernel, outs, args, scratch=(), flops=0, name=None):
    specs = [SMEM if i == 0 else VMEM for i in range(len(args))]
    return pl.pallas_call(
        kernel,
        out_shape=outs,
        in_specs=specs,
        out_specs=jax.tree.map(lambda _: VMEM, outs),
        scratch_shapes=list(scratch),
        compiler_params=PARAMS,
        cost_estimate=pl.CostEstimate(flops=flops, bytes_accessed=10_000_000, transcendentals=0),
        name=name,
    )(*args)


def sds(shape, dtype=BF16):
    return jax.ShapeDtypeStruct(shape, dtype)


def swap(x, axis, k, keep=None):
    n = lax.axis_size(axis)
    return lax.ppermute(x, axis, [(i, i ^ k) for i in range(n) if keep is None or keep(i ^ k)])


def radices(n):
    out = []
    stride = 1
    while stride < n:
        r = 2 if stride == 1 or n // stride < 4 else 4
        out.append((stride, r))
        stride *= r
    return out


def steps_of(order):
    seq = [("seq", s, 2) for s in (1, 2)]
    rows = [("rows", s, r) for s, r in radices(lax.axis_size("rows"))]
    first, rest = rows[0], rows[1:]
    if order == "xy":
        return [seq[0], first, seq[1]] + rest
    return [seq[0], seq[1], first] + rest


def digit(axis, stride, radix):
    return (lax.axis_index(axis) // stride) % radix


def scatter_step(v, axis, stride, radix):
    d = digit(axis, stride, radix)
    total = lax.dynamic_index_in_dim(v, d, 0, keepdims=False).astype(F32)
    for k in range(1, radix):
        part = lax.dynamic_index_in_dim(v, d ^ k, 0, keepdims=False)
        total += swap(part, axis, k * stride).astype(F32)
    return total.astype(BF16)


def gather_step(v, axis, stride, radix):
    d = digit(axis, stride, radix)
    at = lax.broadcasted_iota(jnp.int32, (radix,) + (1,) * v.ndim, 0)
    out = jnp.broadcast_to(v[None], (radix,) + v.shape)
    for k in range(1, radix):
        got = swap(v, axis, k * stride)
        out = jnp.where(at == (d ^ k), got[None], out)
    return out


def sum_all(g, order):
    steps = steps_of(order)
    rows, width = g.shape
    blocks = 1
    for _, _, r in steps:
        blocks *= r
    v = g.reshape(tuple(r for _, _, r in steps) + (rows // blocks, width))
    for s in steps:
        v = scatter_step(v, *s)
    for s in steps[::-1]:
        v = gather_step(v, *s)
    return v.reshape(rows, width)


def shards(
    tokens, seg_ids, w_query, w_key, w_value, w_out, w_gate, w_up, w_down, w_head, norm_attn, norm_ffn,
    bucket_bias_table, grad_y, embedding_gradient,
):
    rows, span, width = tokens.shape
    heads = bucket_bias_table.shape[1]
    buckets = bucket_bias_table.shape[0]
    n = lax.axis_size("seq")
    inner = w_query.shape[1]
    ff = w_gate.shape[1]
    wide = w_head.shape[1]
    length = n * span
    starts = [-(-s * rows // n) for s in range(n + 1)]
    counts = [starts[s + 1] - starts[s] for s in range(n)]
    slots = max(counts)
    assert slots == 3 and min(counts) == 2
    me = lax.axis_index("seq")
    starts_arr = jnp.array(starts[:n], jnp.int32)
    counts_arr = jnp.array(counts, jnp.int32)
    reals = [(counts_arr[me] > j).astype(jnp.int32) for j in range(slots)]
    meta = jnp.stack([me, *reals, starts_arr[me], 0, 0, 0]).astype(jnp.int32)

    seg_low = jnp.pad(seg_ids.astype(BF16)[:, None, :], ((0, 0), (0, 15), (0, width - span)))
    ext = jnp.concatenate([tokens, seg_low], axis=1)

    def spread(array, j):
        out = []
        for k in range(n):
            row = jnp.minimum(starts_arr[me ^ k] + j, rows - 1)
            piece = lax.dynamic_index_in_dim(array, row, 0, keepdims=False)
            out.append(piece if k == 0 else swap(piece, "seq", k, lambda d: counts[d] > j))
        return out

    def collect(pieces):
        got = [
            [p if k == 0 else lax.ppermute(p, "seq", [(i, i ^ k) for i in range(n) if counts[i] > j]) for k, p in enumerate(ps)]
            for j, ps in enumerate(pieces)
        ]
        out = []
        for s in range(n):
            for j in range(counts[s]):
                val = got[j][0]
                for k in range(1, n):
                    val = jnp.where(me == (s ^ k), got[j][k], val)
                out.append(val)
        return jnp.stack(out)

    xs = [spread(ext, j) for j in range(slots)]
    gys = [spread(grad_y, j) for j in range(slots)]

    w_qkv = jnp.concatenate([w_query, w_key, w_value], axis=1)
    wqkv_t, wout_t, wg_t, wu_t, wd_t = w_qkv.T, w_out.T, w_gate.T, w_up.T, w_down.T
    nattn = jnp.broadcast_to(norm_attn[:, None], (width, LANES))
    nffn = jnp.broadcast_to(norm_ffn[:, None], (width, LANES))
    line = 2 * length
    col = jnp.arange(line, dtype=jnp.int32)
    offset = length - span - jnp.where(col < line - span, col, col - line)
    indicator = (bucket_index(offset)[None, :] == jnp.arange(buckets, dtype=jnp.int32)[:, None]).astype(F32)
    lines = jnp.einsum("th,tc->hc", bucket_bias_table, indicator, precision=TOP_PRECISION)
    lines = jnp.pad(lines, ((0, 8 - heads), (0, 0)))
    bias = pl.pallas_call(
        bias_kernel, out_shape=sds((heads, LANES, line), F32), in_specs=[VMEM], out_specs=VMEM, compiler_params=PARAMS,
        name="bias",
    )(lines)

    fwd = []
    for j in range(slots):
        outs = (
            sds((length, inner)), sds((length, inner)), sds((inner, length)), sds((heads, length, length)),
            sds((inner, length)), sds((width, length)), sds((width, length), F32), sds((ff, length)), sds((ff, length)),
            sds((ff, length)), sds((8, width), F32), *[sds((span, width))] * 4,
        )
        scratch = (
            pltpu.VMEM((LANES, length), F32), pltpu.VMEM((width, length), BF16),
            pltpu.VMEM((heads // 2, length, 2 * LANES), BF16), pltpu.VMEM((length, width), F32),
        )
        fwd.append(
            call(
                functools.partial(forward_kernel, j, n), outs,
                (meta, *xs[j], bias, wqkv_t, wout_t, wg_t, wu_t, wd_t, nattn, nffn), scratch, 4_000_000_000, "forward",
            )
        )
    block_out = collect([f[11:15] for f in fwd])

    mids = []
    for j in range(slots):
        outs = (
            sds((width, length)), sds((width, length)), sds((ff, length)), sds((ff, length)), sds((width, length)),
            sds((inner, length)), sds((8, width), F32), sds((8, wide), F32), sds((8, width + wide), F32),
        )
        scratch = (pltpu.VMEM((length, width), F32), pltpu.VMEM((8, length), F32))
        f = fwd[j]
        mids.append(
            call(
                functools.partial(middle_kernel, j, n), outs,
                (meta, *gys[j], *xs[j], embedding_gradient, f[10], f[6], f[7], f[8], w_head, w_down, w_gate, w_up, w_out, nffn),
                scratch, 3_000_000_000, "middle",
            )
        )

    packed_w = 2 * ff + 2 * width + inner
    args = [meta]
    for f, m in zip(fwd, mids):
        args += [f[9], m[1], m[0], m[2], m[3], f[4], m[4]]
    early = call(
        functools.partial(early_grads_kernel, slots - 1), sds((width, packed_w)), args,
        [pltpu.VMEM((width, packed_w), F32)], 6_000_000_000, "early_grads",
    )
    half = (packed_w // 2 // LANES) * LANES
    sums_a = sum_all(early[:, :half], "xy")
    sums_b = sum_all(early[:, half:], "yx")

    back = []
    for j in range(slots):
        outs = (
            sds((width, length)), sds((3 * inner, length)), sds((8, line), F32), sds((8, width), F32),
            *[sds((span, width))] * 4,
        )
        scratch = (pltpu.VMEM((length, length), BF16), pltpu.VMEM((LANES, line), F32), pltpu.VMEM((width, length), F32))
        f, m = fwd[j], mids[j]
        back.append(
            call(
                functools.partial(backward_kernel, j, n), outs,
                (meta, f[0], f[1], f[2], f[3], f[4], f[5], m[5], m[4], w_qkv, nattn), scratch, 4_000_000_000, "backward",
            )
        )
    grad_x = collect([b[4:8] for b in back])
    args = [meta]
    for b in back:
        args += [b[0], b[1]]
    late = call(
        functools.partial(late_grads_kernel, slots - 1), sds((width, 3 * inner)), args,
        [pltpu.VMEM((width, 3 * inner), F32)], 2_000_000_000, "late_grads",
    )

    def total(parts):
        return sum(jnp.where(reals[j] == 1, p, 0.0) for j, p in enumerate(parts))

    gnf = total([m[6][0] for m in mids])
    gna = total([b[3][0] for b in back])
    table_lines = total([b[2][:heads] for b in back])
    table = jnp.einsum("tc,hc->th", indicator, table_lines, precision=TOP_PRECISION)
    small = jnp.concatenate([gnf, gna, table.reshape(-1)])
    small = lax.psum(small, ("rows", "seq"))
    grad_norm_ffn, grad_norm_attn = small[:width], small[width : 2 * width]
    grad_table = small[2 * width :].reshape(buckets, heads)
    sums_c = sum_all(late, "xy")

    emb = jnp.stack([m[7][0] for m in mids])
    emb_all = lax.all_gather(emb, "seq", axis=0)
    embedding = jnp.stack([emb_all[s, j] for s in range(n) for j in range(counts[s])])
    pg = jnp.stack([jnp.where(reals[j] == 1, m[8][0], 0.0) for j, m in enumerate(mids)]).astype(BF16)
    pg_all = lax.all_gather(pg, ("rows", "seq"), axis=0, tiled=True)
    grad_head = lax.dot_general(
        pg_all[:, :width], pg_all[:, width:], (((0,), (0,)), ((), ())), preferred_element_type=F32
    )

    sums = jnp.concatenate([sums_a, sums_b], axis=1).astype(F32)
    grad_gate = sums[:, :ff]
    grad_up = sums[:, ff : 2 * ff]
    grad_down = jnp.concatenate([sums[:, 2 * ff : 2 * ff + width], sums[:, 2 * ff + width : 2 * ff + 2 * width]], axis=0)
    grad_out = sums[:, 2 * ff + 2 * width :].T
    qkv = sums_c.astype(F32)
    return (
        block_out, embedding, grad_x, qkv[:, :inner], qkv[:, inner : 2 * inner], qkv[:, 2 * inner :], grad_out,
        grad_gate, grad_up, grad_down, grad_head, grad_norm_attn, grad_norm_ffn, grad_table,
    )


def solution(mesh):
    by_pos = P("rows", "seq", None)
    by_row = P("rows", None)
    return jax.shard_map(
        shards,
        mesh=mesh,
        in_specs=(by_pos, P("rows", "seq"), *[P()] * 11, by_pos, by_row),
        out_specs=(by_pos, by_row, by_pos, *[P()] * 11),
        check_vma=False,
    )
```

time: 510 us -> 459 us (0.900)
  waiting for transfers between devices: 232 us -> 57.1 us
  Pallas kernels: 0 us -> 133 us
  matrix products: 117 us -> 4.21 us
  starting transfers between devices: 0.38 us -> 85.2 us
  blocking collectives: 57.6 us -> 89.8 us
  local copies, waits for them, and re-layouts: 55.8 us -> 45.3 us
    psum x1 -> x0, waiting for transfers between devices: 172 us -> none  [shards(): lax.psum((grad_query, key_weight_gradient, grad_value, grad_out, grad_gat...]
    pallas_call x0 -> x12, Pallas kernels: none -> 133 us  [the longest x11 129 us: call(): pl.pallas_call(kernel, out_shape=outs, in_specs=specs, out_specs=jax.tree...]
    dot_general x32 -> x3, matrix products: 117 us -> 4.21 us  [the longest x1 2.49 us: shards(): lax.dot_general(pg_all[:, :width], pg_all[:, width:], (((0,), (0,)), ((),...]
    ppermute x0 -> x72, starting transfers between devices: none -> 85.2 us  [the longest x54 62.5 us: swap(): lax.ppermute(x, axis, [(i, i ^ k) for i in range(n) if keep is None or ke...]
    ppermute x0 -> x72, waiting for transfers between devices: none -> 57.1 us  [the longest x54 50.2 us: swap(): lax.ppermute(x, axis, [(i, i ^ k) for i in range(n) if keep is None or ke...]
    all_gather x1 -> x2, blocking collectives: 6.4 us -> 50.1 us  [the longest x1 44.3 us: shards(): pg_all = lax.all_gather(pg, ('rows', 'seq'), axis=0, tiled=True)]
    all_gather x2 -> x0, waiting for transfers between devices: 33.9 us -> none  [the longest x1 17.6 us: shards(): lax.all_gather(k_rows, 'seq', axis=1, tiled=True)]
    reduce_scatter x2 -> x0, waiting for transfers between devices: 25.7 us -> none  [the longest x1 25.7 us: shards(): lax.psum_scatter(key_terms.astype(jnp.bfloat16), 'seq', scatter_dimension...]
  transfers between devices with their start and end apart: 5 -> 72, of which waited for: 4 -> 24; matrix products, arithmetic and copies ran while one was open for 21% -> 12% of each run, Pallas kernels for 0% -> 24%
where the time goes in v1:
time: 459 us; the launch traced here: 454 us
  Pallas kernels  133 us (29%)
  blocking collectives  89.8 us (20%)
  starting transfers between devices  85.2 us (19%)
  waiting for transfers between devices  57.1 us (12%)
  local copies, waits for them, and re-layouts  45.3 us (10%)
  other arithmetic  27.6 us (6%)
  between operations  11.7 us (3%)
    pallas_call x11, Pallas kernels, call(): pl.pallas_call(kernel, out_shape=outs, in_specs=specs, out_specs=jax.tree...  129 us
    ppermute x54, starting transfers between devices, swap(): lax.ppermute(x, axis, [(i, i ^ k) for i in range(n) if keep is None or ke...  62.5 us
    ppermute x54, waiting for transfers between devices, swap(): lax.ppermute(x, axis, [(i, i ^ k) for i in range(n) if keep is None or ke...  50.2 us
    all_gather x1, blocking collectives, shards(): pg_all = lax.all_gather(pg, ('rows', 'seq'), axis=0, tiled=True)  44.3 us
    psum x1, blocking collectives, shards(): small = lax.psum(small, ('rows', 'seq'))  39.6 us
    ppermute x18, starting transfers between devices, collect(): lax.ppermute(p, 'seq', [(i, i ^ k) for i in range(n) if counts[i] > j])  22.8 us
    unnamed x128, local copies, waits for them, and re-layouts  13.2 us
  transfers between devices with their start and end apart: 72, of which 24 were waited for; matrix products, arithmetic and copies ran while one was open for 12% of the time, Pallas kernels for 24%

profile of v1, /device:TPU:0, one launch (start us, length us, event | category | flops | bytes accessed | tf_op | source)
XLA Modules:
  0.0 453.8 jit_solution(4647981005198673373)
XLA Ops:
  14.4 4.9 %collective-permute-start.13 = (bf16[144,512]{1,0:T(8,128)(2,1)}, bf16[144,512]{1,0:T(8,128)(2,1)}, u32[]{:S(2)}, u32[]{:S(2)}) collective-permute-start(bf16[144,512]{1,0:T(8,128)(2,1)} %get-tuple-element.256), channel_id=1, source_target_pairs={{0,2},{2,0},{4,6},{6,4},{8,10},{10,8},{12,14},{14,12},{16,18},{18,... | collective-permute-start | bytes 442376 | tf_op jit(solution)/shard_map/ppermute | solution.py:341
  22.0 2.0 collective-permute-start.7
  37.6 3.4 bias.1
  43.4 2.0 collective-permute-start.1
  47.1 17.2 %forward.5 = (bf16[512,384]{1,0:T(8,128)(2,1)}, bf16[512,384]{1,0:T(8,128)(2,1)}, bf16[384,512]{1,0:T(8,128)(2,1)}, bf16[6,512,512]{2,1,0:T(8,128)(2,1)}, bf16[3...) custom-call(s32[8]{0:T(128)} %stack.89.meta, ...), custom_call_target="tpu_custom_call" | custom-call | flops 4000000000 | bytes 10000000 | tf_op jit(solution)/shard_map/forward/pallas_call | solution.py:323
  65.9 16.9 %forward.4 = (bf16[512,384]{1,0:T(8,128)(2,1)}, bf16[512,384]{1,0:T(8,128)(2,1)}, bf16[384,512]{1,0:T(8,128)(2,1)}, bf16[6,512,512]{2,1,0:T(8,128)(2,1)}, bf16[3...) custom-call(s32[8]{0:T(128)} %stack.89.meta, ...), custom_call_target="tpu_custom_call" | custom-call | flops 4000000000 | bytes 10000000 | tf_op jit(solution)/shard_map/forward/pallas_call | solution.py:323
  82.8 2.8 collective-permute-start.23
  86.9 2.0 collective-permute-start.25
  88.9 17.0 %forward.3 = (bf16[512,384]{1,0:T(8,128)(2,1)}, bf16[512,384]{1,0:T(8,128)(2,1)}, bf16[384,512]{1,0:T(8,128)(2,1)}, bf16[6,512,512]{2,1,0:T(8,128)(2,1)}, bf16[3...) custom-call(s32[8]{0:T(128)} %stack.89.meta, ...), custom_call_target="tpu_custom_call" | custom-call | flops 4000000000 | bytes 10000000 | tf_op jit(solution)/shard_map/forward/pallas_call | solution.py:323
  105.9 2.0 collective-permute-start.22
  108.6 9.4 %middle.5 = (bf16[512,512]{1,0:T(8,128)(2,1)}, bf16[512,512]{1,0:T(8,128)(2,1)}, bf16[1024,512]{1,0:T(8,128)(2,1)}, bf16[1024,512]{1,0:T(8,128)(2,1)}, bf16[512,...) custom-call(s32[8]{0:T(128)} %stack.89.meta, ...), custom_call_target="tpu_custom_call" | custom-call | flops 3000000000 | bytes 10000000 | tf_op jit(solution)/shard_map/middle/pallas_call | solution.py:323
  118.8 9.8 %middle.4 = (bf16[512,512]{1,0:T(8,128)(2,1)}, bf16[512,512]{1,0:T(8,128)(2,1)}, bf16[1024,512]{1,0:T(8,128)(2,1)}, bf16[1024,512]{1,0:T(8,128)(2,1)}, bf16[512,...) custom-call(s32[8]{0:T(128)} %stack.89.meta, ...), custom_call_target="tpu_custom_call" | custom-call | flops 3000000000 | bytes 10000000 | tf_op jit(solution)/shard_map/middle/pallas_call | solution.py:323
  129.3 9.4 %middle.3 = (bf16[512,512]{1,0:T(8,128)(2,1)}, bf16[512,512]{1,0:T(8,128)(2,1)}, bf16[1024,512]{1,0:T(8,128)(2,1)}, bf16[1024,512]{1,0:T(8,128)(2,1)}, bf16[512,...) custom-call(s32[8]{0:T(128)} %stack.89.meta, ...), custom_call_target="tpu_custom_call" | custom-call | flops 3000000000 | bytes 10000000 | tf_op jit(solution)/shard_map/middle/pallas_call | solution.py:323
  138.8 13.7 %early_grads.1 = bf16[512,3456]{1,0:T(8,128)(2,1)} custom-call(s32[8]{0:T(128)} %stack.89.meta, bf16[1024,512]{1,0:T(8,128)(2,1)} %get-tuple-element.179.refs_0_, bf16[512,512]{1,0:T(8,128)(2,1)} %get-tuple-element.180.refs_1_, bf16[512,512]{1,0:T(8,128)(2,1)} %get-tuple-element.181.refs_2_, bf16[1024,512]{1,0:T(8,128)(2,1)} %get-tuple-element.182.refs_3_, ...), custom_call_target="tpu_custom_call" | custom-call | flops 6000000000 | bytes 10000000 | tf_op jit(solution)/shard_map/early_grads/pallas_call | solution.py:323
  155.7 2.0 collective-permute-start.15
  157.6 3.3 collective-permute-start.16
  169.7 10.1 %backward.5 = (bf16[512,512]{1,0:T(8,128)(2,1)}, bf16[1152,512]{1,0:T(8,128)(2,1)}, f32[8,1024]{1,0:T(8,128)}, f32[8,512]{1,0:T(8,128)}, bf16[128,512]{1,0:T(8,1...) custom-call(s32[8]{0:T(128)} %stack.89.meta, ...), custom_call_target="tpu_custom_call" | custom-call | flops 4000000000 | bytes 10000000 | tf_op jit(solution)/shard_map/backward/pallas_call | solution.py:323
  179.8 9.9 %backward.4 = (bf16[512,512]{1,0:T(8,128)(2,1)}, bf16[1152,512]{1,0:T(8,128)(2,1)}, f32[8,1024]{1,0:T(8,128)}, f32[8,512]{1,0:T(8,128)}, bf16[128,512]{1,0:T(8,1...) custom-call(s32[8]{0:T(128)} %stack.89.meta, ...), custom_call_target="tpu_custom_call" | custom-call | flops 4000000000 | bytes 10000000 | tf_op jit(solution)/shard_map/backward/pallas_call | solution.py:323
  189.7 10.1 %backward.3 = (bf16[512,512]{1,0:T(8,128)(2,1)}, bf16[1152,512]{1,0:T(8,128)(2,1)}, f32[8,1024]{1,0:T(8,128)}, f32[8,512]{1,0:T(8,128)}, bf16[128,512]{1,0:T(8,1...) custom-call(s32[8]{0:T(128)} %stack.89.meta, ...), custom_call_target="tpu_custom_call" | custom-call | flops 4000000000 | bytes 10000000 | tf_op jit(solution)/shard_map/backward/pallas_call | solution.py:323
  205.0 39.6 %psum.7 = f32[1216]{0:T(1024)} all-reduce(f32[1216]{0:T(1024)S(1)} %pad_maximum_fusion.1), channel_id=1, replica_groups=mesh['rows'=8,'seq'=4] {'rows','seq'}, use_global_device_ids=true, to_apply=%region_0.1 | all-reduce | flops 1216 | bytes 9728 | tf_op jit(solution)/shard_map/psum | solution.py:543
  248.1 5.8 %all-gather.1 = f32[4,3,768]{2,1,0:T(4,128)S(1)} all-gather(f32[1,3,768]{2,1,0:T(4,128)S(1)} %maximum_bitcast_fusion), channel_id=2, replica_groups=mesh['rows'=8,'seq'=4] {'seq'}, dimensions={0}, use_global_device_ids=true | all-gather | bytes 46080 | tf_op jit(solution)/shard_map/all_gather | solution.py:549
  255.3 44.3 %all-gather.2 = bf16[32,3,1280]{2,1,0:T(4,128)(2,1)} all-gather(bf16[1,3,1280]{2,1,0:T(4,128)(2,1)S(1)} %maximum_bitcast_fusion.1), channel_id=1, replica_groups=mesh['rows'=8,'seq'=4] {'rows','seq'}, dimensions={0}, use_global_device_ids=true | all-gather | bytes 253440 | tf_op jit(solution)/shard_map/all_gather | solution.py:552
  301.5 2.5 fusion.12
  304.0 6.0 %late_grads.1 = bf16[512,1152]{1,0:T(8,128)(2,1)} custom-call(s32[8]{0:T(128)} %stack.89.meta, bf16[512,512]{1,0:T(8,128)(2,1)} %get-tuple-element.173.n1_0, bf16[1152,512]{1,0:T(8,128)(2,1)} %get-tuple-element.174.g_0, bf16[512,512]{1,0:T(8,128)(2,1)} %get-tuple-element.175.n1_1, bf16[1152,512]{1,0:T(8,128)(2,1)} %get-tuple-element.176.g_1, ...), custom_call_target="tpu_custom_call" | custom-call | flops 2000000000 | bytes 10000000 | tf_op jit(solution)/shard_map/late_grads/pallas_call | solution.py:323
  313.9 2.0 stack.102
  319.4 3.1 collective-permute-done.9
  326.3 4.0 collective-permute-start.34
  339.1 2.5 collective-permute-start.31
  348.3 8.9 %collective-permute-done.37 = bf16[2,4,16,1152]{3,2,1,0:T(8,128)(2,1)S(1)} collective-permute-done((bf16[2,4,16,1152]{3,2,1,0:T(8,128)(2,1)S(1)}, bf16[2,4,16,1152]{3,2,1,0:T(8,128)(2,1)S(1)}, u32[]{:S(2)}, u32[]{:S(2)}) %collective-permute-start.37) | collective-permute-done | bytes 294944 | tf_op jit(solution)/shard_map/ppermute | solution.py:341
  358.8 3.7 collective-permute-done.38
  362.7 3.4 collective-permute-start.40
  369.7 2.5 collective-permute-start.43
  374.5 3.4 collective-permute-done.42
  380.2 4.7 %collective-permute-done.45 = bf16[4,16,1152]{2,1,0:T(8,128)(2,1)S(1)} collective-permute-done((bf16[4,16,1152]{2,1,0:T(8,128)(2,1)S(1)}, bf16[4,16,1152]{2,1,0:T(8,128)(2,1)S(1)}, u32[]{:S(2)}, u32[]{:S(2)}) %collective-permute-start.45) | collective-permute-done | bytes 147488 | tf_op jit(solution)/shard_map/ppermute | solution.py:341
  386.9 4.2 collective-permute-done.61
  391.3 2.2 collective-permute-done.50
  395.1 2.0 collective-permute-start.52
  397.1 2.4 collective-permute-start.62
  400.0 2.2 collective-permute-done.52
  404.6 2.2 collective-permute-start.65
  408.5 2.4 collective-permute-start.54
  414.9 2.1 collective-permute-start.66
  421.0 2.6 collective-permute-start.69
  425.6 4.5 collective-permute-done.69
  431.5 4.4 collective-permute-done.58
  436.2 2.6 collective-permute-done.70
  442.7 3.4 maximum_convert_fusion
  447.2 4.8 %fusion.58 = (f32[512,1024]{1,0:T(8,128)}, f32[512,1024]{1,0:T(8,128)}) fusion(f32[512,3456]{1,0:T(8,128)} %maximum_convert_fusion), kind=kLoop, calls=%fused_computation.186 | loop fusion | bytes 8388608 | tf_op jit(solution)/shard_map/slice | solution.py:559
  (344 shorter events, 116.0 us)
Async XLA Ops:
  13.1 30.1 %collective-permute-start.14 = (bf16[144,512]{1,0:T(8,128)(2,1)}, bf16[144,512]{1,0:T(8,128)(2,1)}, u32[]{:S(2)}, u32[]{:S(2)}) collective-permute-start(bf16[144,512]{1,0:T(8,128)(2,1)} %get-tuple-element.255), channel_id=1, source_target_pairs={{1,2},{3,0},{5,6},{7,4},{9,10},{11,8},{13,14},{15,12},{17,18},{19,... | collective-permute-start | bytes 442376 | tf_op jit(solution)/shard_map/ppermute | solution.py:341
  14.4 28.8 %collective-permute-start.13 = (bf16[144,512]{1,0:T(8,128)(2,1)}, bf16[144,512]{1,0:T(8,128)(2,1)}, u32[]{:S(2)}, u32[]{:S(2)}) collective-permute-start(bf16[144,512]{1,0:T(8,128)(2,1)} %get-tuple-element.256), channel_id=1, source_target_pairs={{0,2},{2,0},{4,6},{6,4},{8,10},{10,8},{12,14},{14,12},{16,18},{18,... | collective-permute-start | bytes 442376 | tf_op jit(solution)/shard_map/ppermute | solution.py:341
  19.3 24.1 %collective-permute-start.12 = (bf16[144,512]{1,0:T(8,128)(2,1)}, bf16[144,512]{1,0:T(8,128)(2,1)}, u32[]{:S(2)}, u32[]{:S(2)}) collective-permute-start(bf16[144,512]{1,0:T(8,128)(2,1)} %get-tuple-element.257), channel_id=1, source_target_pairs={{1,0},{3,2},{5,4},{7,6},{9,8},{11,10},{13,12},{15,14},{17,16},{19,... | collective-permute-start | bytes 442376 | tf_op jit(solution)/shard_map/ppermute | solution.py:341
  20.6 43.7 %collective-permute-start.8 = (bf16[144,512]{1,0:T(8,128)(2,1)}, bf16[144,512]{1,0:T(8,128)(2,1)}, u32[]{:S(2)}, u32[]{:S(2)}) collective-permute-start(bf16[144,512]{1,0:T(8,128)(2,1)} %get-tuple-element.259), channel_id=1, source_target_pairs={{0,3},{1,2},{2,1},{3,0},{4,7},{5,6},{6,5},{7,4},{8,11},{9,10},{10,... | collective-permute-start | bytes 442376 | tf_op jit(solution)/shard_map/ppermute | solution.py:341
  22.0 42.4 %collective-permute-start.7 = (bf16[144,512]{1,0:T(8,128)(2,1)}, bf16[144,512]{1,0:T(8,128)(2,1)}, u32[]{:S(2)}, u32[]{:S(2)}) collective-permute-start(bf16[144,512]{1,0:T(8,128)(2,1)} %get-tuple-element.260), channel_id=1, source_target_pairs={{0,2},{1,3},{2,0},{3,1},{4,6},{5,7},{6,4},{7,5},{8,10},{9,11},{10,... | collective-permute-start | bytes 442376 | tf_op jit(solution)/shard_map/ppermute | solution.py:341
  43.2 21.3 %collective-permute-start.6 = (bf16[144,512]{1,0:T(8,128)(2,1)S(1)}, bf16[144,512]{1,0:T(8,128)(2,1)S(1)}, u32[]{:S(2)}, u32[]{:S(2)}) collective-permute-start(bf16[144,512]{1,0:T(8,128)(2,1)S(1)} %copy-done.24), channel_id=1, source_target_pairs={{0,1},{1,0},{2,3},{3,2},{4,5},{5,4},{6,7},{7,6},{8,9},{9,8},{10,11... | collective-permute-start | bytes 442376 | tf_op jit(solution)/shard_map/ppermute | solution.py:341
  43.3 39.5 %collective-permute-start.2 = (bf16[144,512]{1,0:T(8,128)(2,1)S(1)}, bf16[144,512]{1,0:T(8,128)(2,1)S(1)}, u32[]{:S(2)}, u32[]{:S(2)}) collective-permute-start(bf16[144,512]{1,0:T(8,128)(2,1)S(1)} %copy-done.23), channel_id=1, source_target_pairs={{0,3},{1,2},{2,1},{3,0},{4,7},{5,6},{6,5},{7,4},{8,11},{9,10},{10,... | collective-permute-start | bytes 442376 | tf_op jit(solution)/shard_map/ppermute | solution.py:341
  43.4 42.1 %collective-permute-start.1 = (bf16[144,512]{1,0:T(8,128)(2,1)S(1)}, bf16[144,512]{1,0:T(8,128)(2,1)S(1)}, u32[]{:S(2)}, u32[]{:S(2)}) collective-permute-start(bf16[144,512]{1,0:T(8,128)(2,1)S(1)} %copy-done.22), channel_id=1, source_target_pairs={{0,2},{1,3},{2,0},{3,1},{4,6},{5,7},{6,4},{7,5},{8,10},{9,11},{10,... | collective-permute-start | bytes 442376 | tf_op jit(solution)/shard_map/ppermute | solution.py:341
  64.3 22.5 %collective-permute-start = (bf16[144,512]{1,0:T(8,128)(2,1)S(1)}, bf16[144,512]{1,0:T(8,128)(2,1)S(1)}, u32[]{:S(2)}, u32[]{:S(2)}) collective-permute-start(bf16[144,512]{1,0:T(8,128)(2,1)S(1)} %copy-done.21), channel_id=1, source_target_pairs={{0,1},{1,0},{2,3},{3,2},{4,5},{5,4},{6,7},{7,6},{8,9},{9,8},{10,11... | collective-permute-start | bytes 442376 | tf_op jit(solution)/shard_map/ppermute | solution.py:341
  64.4 64.2 %collective-permute-start.20 = (bf16[128,512]{1,0:T(8,128)(2,1)S(1)}, bf16[128,512]{1,0:T(8,128)(2,1)S(1)}, u32[]{:S(2)}, u32[]{:S(2)}) collective-permute-start(bf16[128,512]{1,0:T(8,128)(2,1)S(1)} %get-tuple-element.267), channel_id=1, source_target_pairs={{0,3},{1,2},{2,1},{3,0},{4,7},{5,6},{6,5},{7,4},{8,11},{9,10},{10,... | collective-permute-start | bytes 393224 | tf_op jit(solution)/shard_map/ppermute | solution.py:341
  64.6 41.3 %collective-permute-start.24 = (bf16[128,512]{1,0:T(8,128)(2,1)S(1)}, bf16[128,512]{1,0:T(8,128)(2,1)S(1)}, u32[]{:S(2)}, u32[]{:S(2)}) collective-permute-start(bf16[128,512]{1,0:T(8,128)(2,1)S(1)} %get-tuple-element.268), channel_id=1, source_target_pairs={{1,0},{3,2},{5,4},{7,6},{9,8},{11,10},{13,12},{15,14},{17,16},{19,... | collective-permute-start | bytes 393224 | tf_op jit(solution)/shard_map/ppermute | solution.py:341
  82.8 35.2 %collective-permute-start.23 = (bf16[128,512]{1,0:T(8,128)(2,1)S(1)}, bf16[128,512]{1,0:T(8,128)(2,1)S(1)}, u32[]{:S(2)}, u32[]{:S(2)}) collective-permute-start(bf16[128,512]{1,0:T(8,128)(2,1)S(1)} %get-tuple-element.270), channel_id=1, source_target_pairs={{0,3},{1,2},{2,1},{3,0},{4,7},{5,6},{6,5},{7,4},{8,11},{9,10},{10,... | collective-permute-start | bytes 393224 | tf_op jit(solution)/shard_map/ppermute | solution.py:341
  85.5 22.4 %collective-permute-start.26 = (bf16[128,512]{1,0:T(8,128)(2,1)S(1)}, bf16[128,512]{1,0:T(8,128)(2,1)S(1)}, u32[]{:S(2)}, u32[]{:S(2)}) collective-permute-start(bf16[128,512]{1,0:T(8,128)(2,1)S(1)} %get-tuple-element.277), channel_id=1, source_target_pairs={{1,2},{3,0},{5,6},{7,4},{9,10},{11,8},{13,14},{15,12},{17,18},{19,... | collective-permute-start | bytes 393224 | tf_op jit(solution)/shard_map/ppermute | solution.py:341
  86.9 21.1 %collective-permute-start.25 = (bf16[128,512]{1,0:T(8,128)(2,1)S(1)}, bf16[128,512]{1,0:T(8,128)(2,1)S(1)}, u32[]{:S(2)}, u32[]{:S(2)}) collective-permute-start(bf16[128,512]{1,0:T(8,128)(2,1)S(1)} %get-tuple-element.278), channel_id=1, source_target_pairs={{0,2},{2,0},{4,6},{6,4},{8,10},{10,8},{12,14},{14,12},{16,18},{18,... | collective-permute-start | bytes 393224 | tf_op jit(solution)/shard_map/ppermute | solution.py:341
  105.9 12.2 %collective-permute-start.22 = (bf16[128,512]{1,0:T(8,128)(2,1)S(1)}, bf16[128,512]{1,0:T(8,128)(2,1)S(1)}, u32[]{:S(2)}, u32[]{:S(2)}) collective-permute-start(bf16[128,512]{1,0:T(8,128)(2,1)S(1)} %get-tuple-element.271), channel_id=1, source_target_pairs={{0,2},{1,3},{2,0},{3,1},{4,6},{5,7},{6,4},{7,5},{8,10},{9,11},{10,... | collective-permute-start | bytes 393224 | tf_op jit(solution)/shard_map/ppermute | solution.py:341
  107.9 10.2 %collective-permute-start.21 = (bf16[128,512]{1,0:T(8,128)(2,1)S(1)}, bf16[128,512]{1,0:T(8,128)(2,1)S(1)}, u32[]{:S(2)}, u32[]{:S(2)}) collective-permute-start(bf16[128,512]{1,0:T(8,128)(2,1)S(1)} %get-tuple-element.272), channel_id=1, source_target_pairs={{0,1},{1,0},{2,3},{3,2},{4,5},{5,4},{6,7},{7,6},{8,9},{9,8},{10,11... | collective-permute-start | bytes 393224 | tf_op jit(solution)/shard_map/ppermute | solution.py:341
  107.9 20.6 %collective-permute-start.19 = (bf16[128,512]{1,0:T(8,128)(2,1)S(1)}, bf16[128,512]{1,0:T(8,128)(2,1)S(1)}, u32[]{:S(2)}, u32[]{:S(2)}) collective-permute-start(bf16[128,512]{1,0:T(8,128)(2,1)S(1)} %get-tuple-element.274), channel_id=1, source_target_pairs={{0,2},{1,3},{2,0},{3,1},{4,6},{5,7},{6,4},{7,5},{8,10},{9,11},{10,... | collective-permute-start | bytes 393224 | tf_op jit(solution)/shard_map/ppermute | solution.py:341
  118.0 10.6 %collective-permute-start.18 = (bf16[128,512]{1,0:T(8,128)(2,1)S(1)}, bf16[128,512]{1,0:T(8,128)(2,1)S(1)}, u32[]{:S(2)}, u32[]{:S(2)}) collective-permute-start(bf16[128,512]{1,0:T(8,128)(2,1)S(1)} %get-tuple-element.275), channel_id=1, source_target_pairs={{0,1},{1,0},{2,3},{3,2},{4,5},{5,4},{6,7},{7,6},{8,9},{9,8},{10,11... | collective-permute-start | bytes 393224 | tf_op jit(solution)/shard_map/ppermute | solution.py:341
  155.7 175.6 %collective-permute-start.15 = (bf16[128,512]{1,0:T(8,128)(2,1)}, bf16[128,512]{1,0:T(8,128)(2,1)}, u32[]{:S(2)}, u32[]{:S(2)}) collective-permute-start(bf16[128,512]{1,0:T(8,128)(2,1)} %get-tuple-element.118), channel_id=1, source_target_pairs={{0,3},{2,1},{4,7},{6,5},{8,11},{10,9},{12,15},{14,13},{16,19},{18,... | collective-permute-start | bytes 393224 | tf_op jit(solution)/shard_map/ppermute | solution.py:435
  157.6 173.7 %collective-permute-start.16 = (bf16[128,512]{1,0:T(8,128)(2,1)}, bf16[128,512]{1,0:T(8,128)(2,1)}, u32[]{:S(2)}, u32[]{:S(2)}) collective-permute-start(bf16[128,512]{1,0:T(8,128)(2,1)} %get-tuple-element.119), channel_id=1, source_target_pairs={{0,2},{2,0},{4,6},{6,4},{8,10},{10,8},{12,14},{14,12},{16,18},{18,... | collective-permute-start | bytes 393224 | tf_op jit(solution)/shard_map/ppermute | solution.py:435
  162.4 154.1 %collective-permute-start.3 = (bf16[128,512]{1,0:T(8,128)(2,1)}, bf16[128,512]{1,0:T(8,128)(2,1)}, u32[]{:S(2)}, u32[]{:S(2)}) collective-permute-start(bf16[128,512]{1,0:T(8,128)(2,1)} %get-tuple-element.110), channel_id=1, source_target_pairs={{0,3},{1,2},{2,1},{3,0},{4,7},{5,6},{6,5},{7,4},{8,11},{9,10},{10,... | collective-permute-start | bytes 393224 | tf_op jit(solution)/shard_map/ppermute | solution.py:435
  162.4 154.1 %collective-permute-start.4 = (bf16[128,512]{1,0:T(8,128)(2,1)}, bf16[128,512]{1,0:T(8,128)(2,1)}, u32[]{:S(2)}, u32[]{:S(2)}) collective-permute-start(bf16[128,512]{1,0:T(8,128)(2,1)} %get-tuple-element.111), channel_id=1, source_target_pairs={{0,2},{1,3},{2,0},{3,1},{4,6},{5,7},{6,4},{7,5},{8,10},{9,11},{10,... | collective-permute-start | bytes 393224 | tf_op jit(solution)/shard_map/ppermute | solution.py:435
  163.1 154.5 %collective-permute-start.5 = (bf16[128,512]{1,0:T(8,128)(2,1)}, bf16[128,512]{1,0:T(8,128)(2,1)}, u32[]{:S(2)}, u32[]{:S(2)}) collective-permute-start(bf16[128,512]{1,0:T(8,128)(2,1)} %get-tuple-element.112), channel_id=1, source_target_pairs={{0,1},{1,0},{2,3},{3,2},{4,5},{5,4},{6,7},{7,6},{8,9},{9,8},{10,11... | collective-permute-start | bytes 393224 | tf_op jit(solution)/shard_map/ppermute | solution.py:435
  316.5 8.1 %collective-permute-start.10 = (bf16[128,512]{1,0:T(8,128)(2,1)}, bf16[128,512]{1,0:T(8,128)(2,1)S(1)}, u32[]{:S(2)}, u32[]{:S(2)}) collective-permute-start(bf16[128,512]{1,0:T(8,128)(2,1)} %get-tuple-element.115), channel_id=1, source_target_pairs={{0,2},{1,3},{2,0},{3,1},{4,6},{5,7},{6,4},{7,5},{8,10},{9,11},{10,... | collective-permute-start | bytes 393224 | tf_op jit(solution)/shard_map/ppermute | solution.py:435
  317.6 8.6 %collective-permute-start.11 = (bf16[128,512]{1,0:T(8,128)(2,1)}, bf16[128,512]{1,0:T(8,128)(2,1)S(1)}, u32[]{:S(2)}, u32[]{:S(2)}) collective-permute-start(bf16[128,512]{1,0:T(8,128)(2,1)} %get-tuple-element.116), channel_id=1, source_target_pairs={{0,1},{1,0},{2,3},{3,2},{4,5},{5,4},{6,7},{7,6},{8,9},{9,8},{10,11... | collective-permute-start | bytes 393224 | tf_op jit(solution)/shard_map/ppermute | solution.py:435
  322.5 8.9 %collective-permute-start.17 = (bf16[128,512]{1,0:T(8,128)(2,1)}, bf16[128,512]{1,0:T(8,128)(2,1)S(1)}, u32[]{:S(2)}, u32[]{:S(2)}) collective-permute-start(bf16[128,512]{1,0:T(8,128)(2,1)} %get-tuple-element.120), channel_id=1, source_target_pairs={{0,1},{2,3},{4,5},{6,7},{8,9},{10,11},{12,13},{14,15},{16,17},{18,... | collective-permute-start | bytes 393224 | tf_op jit(solution)/shard_map/ppermute | solution.py:435
  324.6 21.9 %collective-permute-start.33 = (bf16[128,512]{1,0:T(8,128)(2,1)}, bf16[128,512]{1,0:T(8,128)(2,1)S(1)}, u32[]{:S(2)}, u32[]{:S(2)}) collective-permute-start(bf16[128,512]{1,0:T(8,128)(2,1)} %get-tuple-element.169), channel_id=1, source_target_pairs={{0,3},{2,1},{4,7},{6,5},{8,11},{10,9},{12,15},{14,13},{16,19},{18,... | collective-permute-start | bytes 393224 | tf_op jit(solution)/shard_map/ppermute | solution.py:435
  326.3 20.4 %collective-permute-start.34 = (bf16[128,512]{1,0:T(8,128)(2,1)}, bf16[128,512]{1,0:T(8,128)(2,1)S(1)}, u32[]{:S(2)}, u32[]{:S(2)}) collective-permute-start(bf16[128,512]{1,0:T(8,128)(2,1)} %get-tuple-element.170), channel_id=1, source_target_pairs={{0,2},{2,0},{4,6},{6,4},{8,10},{10,8},{12,14},{14,12},{16,18},{18,... | collective-permute-start | bytes 393224 | tf_op jit(solution)/shard_map/ppermute | solution.py:435
  331.4 7.8 %collective-permute-start.28 = (bf16[128,512]{1,0:T(8,128)(2,1)S(1)}, bf16[128,512]{1,0:T(8,128)(2,1)S(1)}, u32[]{:S(2)}, u32[]{:S(2)}) collective-permute-start(bf16[128,512]{1,0:T(8,128)(2,1)S(1)} %copy-done.45), channel_id=1, source_target_pairs={{0,2},{1,3},{2,0},{3,1},{4,6},{5,7},{6,4},{7,5},{8,10},{9,11},{10,... | collective-permute-start | bytes 393224 | tf_op jit(solution)/shard_map/ppermute | solution.py:435
  331.5 10.1 %collective-permute-start.29 = (bf16[128,512]{1,0:T(8,128)(2,1)S(1)}, bf16[128,512]{1,0:T(8,128)(2,1)S(1)}, u32[]{:S(2)}, u32[]{:S(2)}) collective-permute-start(bf16[128,512]{1,0:T(8,128)(2,1)S(1)} %copy-done.44), channel_id=1, source_target_pairs={{0,1},{1,0},{2,3},{3,2},{4,5},{5,4},{6,7},{7,6},{8,9},{9,8},{10,11... | collective-permute-start | bytes 393224 | tf_op jit(solution)/shard_map/ppermute | solution.py:435
  339.1 6.7 %collective-permute-start.31 = (bf16[128,512]{1,0:T(8,128)(2,1)S(1)}, bf16[128,512]{1,0:T(8,128)(2,1)S(1)}, u32[]{:S(2)}, u32[]{:S(2)}) collective-permute-start(bf16[128,512]{1,0:T(8,128)(2,1)S(1)} %copy-done.42), channel_id=1, source_target_pairs={{0,2},{1,3},{2,0},{3,1},{4,6},{5,7},{6,4},{7,5},{8,10},{9,11},{10,... | collective-permute-start | bytes 393224 | tf_op jit(solution)/shard_map/ppermute | solution.py:435
  345.9 12.7 %collective-permute-start.48 = (bf16[2,2,4,16,1664]{4,3,2,1,0:T(8,128)(2,1)S(1)}, bf16[2,2,4,16,1664]{4,3,2,1,0:T(8,128)(2,1)S(1)}, u32[]{:S(2)}, u32[]{:S(2)}) collective-permute-start(bf16[2,2,4,16,1664]{4,3,2,1,0:T(8,128)(2,1)S(1)} %copy-done.13), channel_id=1, source_target_pairs={{0,1},{1,0},{2,3},{3,2},{4,5},{5,4},{6,7},{7,6},{8,9},{9,8},{10,11... | collective-permute-start | bytes 2555912 | tf_op jit(solution)/shard_map/ppermute | solution.py:341
  346.5 27.2 %collective-permute-start.60 = (bf16[2,2,4,16,1792]{4,3,2,1,0:T(8,128)(2,1)S(1)}, bf16[2,2,4,16,1792]{4,3,2,1,0:T(8,128)(2,1)S(1)}, u32[]{:S(2)}, u32[]{:S(2)}) collective-permute-start(bf16[2,2,4,16,1792]{4,3,2,1,0:T(8,128)(2,1)S(1)} %copy-done.12), channel_id=1, source_target_pairs={{0,1},{1,0},{2,3},{3,2},{4,5},{5,4},{6,7},{7,6},{8,9},{9,8},{10,11... | collective-permute-start | bytes 2752520 | tf_op jit(solution)/shard_map/ppermute | solution.py:341
  348.1 9.1 %collective-permute-start.37 = (bf16[2,4,16,1152]{3,2,1,0:T(8,128)(2,1)S(1)}, bf16[2,4,16,1152]{3,2,1,0:T(8,128)(2,1)S(1)}, u32[]{:S(2)}, u32[]{:S(2)}) collective-permute-start(bf16[2,4,16,1152]{3,2,1,0:T(8,128)(2,1)S(1)} %dynamic-slice_bitcast_fusion.5), channel_id=1, source_target_pairs={{0,4},{4,0},{8,12},{12,8},{16,20},{20,16},{24,28},{28,24},{1,5},{5... | collective-permute-start | bytes 884744 | tf_op jit(solution)/shard_map/ppermute | solution.py:341
  366.2 19.4 %collective-permute-start.49 = (bf16[2,4,16,1664]{3,2,1,0:T(8,128)(2,1)S(1)}, bf16[2,4,16,1664]{3,2,1,0:T(8,128)(2,1)S(1)}, u32[]{:S(2)}, u32[]{:S(2)}) collective-permute-start(bf16[2,4,16,1664]{3,2,1,0:T(8,128)(2,1)S(1)} %dynamic-slice_bitcast_fusion.4), channel_id=1, source_target_pairs={{0,4},{4,0},{8,12},{12,8},{16,20},{20,16},{24,28},{28,24},{1,5},{5... | collective-permute-start | bytes 1277960 | tf_op jit(solution)/shard_map/ppermute | solution.py:341
  378.0 6.9 %collective-permute-start.45 = (bf16[4,16,1152]{2,1,0:T(8,128)(2,1)S(1)}, bf16[4,16,1152]{2,1,0:T(8,128)(2,1)S(1)}, u32[]{:S(2)}, u32[]{:S(2)}) collective-permute-start(bf16[4,16,1152]{2,1,0:T(8,128)(2,1)S(1)} %select_select_fusion.2), channel_id=1, source_target_pairs={{0,2},{1,3},{2,0},{3,1},{4,6},{5,7},{6,4},{7,5},{8,10},{9,11},{10,... | collective-permute-start | bytes 442376 | tf_op jit(solution)/shard_map/ppermute | solution.py:341
  379.3 11.8 %collective-permute-start.61 = (bf16[2,4,16,1792]{3,2,1,0:T(8,128)(2,1)S(1)}, bf16[2,4,16,1792]{3,2,1,0:T(8,128)(2,1)S(1)}, u32[]{:S(2)}, u32[]{:S(2)}) collective-permute-start(bf16[2,4,16,1792]{3,2,1,0:T(8,128)(2,1)S(1)} %dynamic-slice_bitcast_fusion.3), channel_id=1, source_target_pairs={{0,2},{1,3},{2,0},{3,1},{4,6},{5,7},{6,4},{7,5},{8,10},{9,11},{10,... | collective-permute-start | bytes 1376264 | tf_op jit(solution)/shard_map/ppermute | solution.py:341
  385.0 21.9 %collective-permute-start.46 = (bf16[2,4,16,1152]{3,2,1,0:T(8,128)(2,1)S(1)}, bf16[2,4,16,1152]{3,2,1,0:T(8,128)(2,1)S(1)}, u32[]{:S(2)}, u32[]{:S(2)}) collective-permute-start(bf16[2,4,16,1152]{3,2,1,0:T(8,128)(2,1)S(1)} %broadcast_select_fusion.5), channel_id=1, source_target_pairs={{0,4},{4,0},{8,12},{12,8},{16,20},{20,16},{24,28},{28,24},{1,5},{5... | collective-permute-start | bytes 884744 | tf_op jit(solution)/shard_map/ppermute | solution.py:341
  385.7 7.8 %collective-permute-start.50 = (bf16[4,16,1664]{2,1,0:T(8,128)(2,1)S(1)}, bf16[4,16,1664]{2,1,0:T(8,128)(2,1)S(1)}, u32[]{:S(2)}, u32[]{:S(2)}) collective-permute-start(bf16[4,16,1664]{2,1,0:T(8,128)(2,1)S(1)} %dynamic-slice_bitcast_fusion.7), channel_id=1, source_target_pairs={{0,2},{1,3},{2,0},{3,1},{4,6},{5,7},{6,4},{7,5},{8,10},{9,11},{10,... | collective-permute-start | bytes 638984 | tf_op jit(solution)/shard_map/ppermute | solution.py:341
  395.1 7.0 %collective-permute-start.52 = (bf16[16,1664]{1,0:T(8,128)(2,1)S(1)}, bf16[16,1664]{1,0:T(8,128)(2,1)S(1)}, u32[]{:S(2)}, u32[]{:S(2)}) collective-permute-start(bf16[16,1664]{1,0:T(8,128)(2,1)S(1)} %get-tuple-element.284), channel_id=1, source_target_pairs={{0,16},{4,20},{8,24},{12,28},{16,0},{20,4},{24,8},{28,12},{1,17},{... | collective-permute-start | bytes 159752 | tf_op jit(solution)/shard_map/ppermute | solution.py:341
  397.1 6.7 %collective-permute-start.62 = (bf16[4,16,1792]{2,1,0:T(8,128)(2,1)S(1)}, bf16[4,16,1792]{2,1,0:T(8,128)(2,1)S(1)}, u32[]{:S(2)}, u32[]{:S(2)}) collective-permute-start(bf16[4,16,1792]{2,1,0:T(8,128)(2,1)S(1)} %dynamic-slice_bitcast_fusion.6), channel_id=1, source_target_pairs={{0,4},{4,0},{8,12},{12,8},{16,20},{20,16},{24,28},{28,24},{1,5},{5... | collective-permute-start | bytes 688136 | tf_op jit(solution)/shard_map/ppermute | solution.py:341
  402.2 11.0 %collective-permute-start.56 = (bf16[16,1664]{1,0:T(8,128)(2,1)S(1)}, bf16[16,1664]{1,0:T(8,128)(2,1)S(1)}, u32[]{:S(2)}, u32[]{:S(2)}) collective-permute-start(bf16[16,1664]{1,0:T(8,128)(2,1)S(1)} %fusion.20), channel_id=1, source_target_pairs={{0,8},{4,12},{8,0},{12,4},{16,24},{20,28},{24,16},{28,20},{1,9},{5... | collective-permute-start | bytes 159752 | tf_op jit(solution)/shard_map/ppermute | solution.py:341
  402.2 12.7 %collective-permute-start.55 = (bf16[16,1664]{1,0:T(8,128)(2,1)S(1)}, bf16[16,1664]{1,0:T(8,128)(2,1)S(1)}, u32[]{:S(2)}, u32[]{:S(2)}) collective-permute-start(bf16[16,1664]{1,0:T(8,128)(2,1)S(1)} %fusion.20), channel_id=1, source_target_pairs={{0,16},{4,20},{8,24},{12,28},{16,0},{20,4},{24,8},{28,12},{1,17},{... | collective-permute-start | bytes 159752 | tf_op jit(solution)/shard_map/ppermute | solution.py:341
  408.5 8.5 %collective-permute-start.54 = (bf16[16,1664]{1,0:T(8,128)(2,1)S(1)}, bf16[16,1664]{1,0:T(8,128)(2,1)S(1)}, u32[]{:S(2)}, u32[]{:S(2)}) collective-permute-start(bf16[16,1664]{1,0:T(8,128)(2,1)S(1)} %fusion.20), channel_id=1, source_target_pairs={{0,24},{4,28},{8,16},{12,20},{16,8},{20,12},{24,0},{28,4},{1,25},{... | collective-permute-start | bytes 159752 | tf_op jit(solution)/shard_map/ppermute | solution.py:341
  411.0 28.3 %collective-permute-start.47 = (bf16[2,2,4,16,1152]{4,3,2,1,0:T(8,128)(2,1)S(1)}, bf16[2,2,4,16,1152]{4,3,2,1,0:T(8,128)(2,1)S(1)}, u32[]{:S(2)}, u32[]{:S(2)}) collective-permute-start(bf16[2,2,4,16,1152]{4,3,2,1,0:T(8,128)(2,1)S(1)} %broadcast_select_fusion.2), channel_id=1, source_target_pairs={{0,1},{1,0},{2,3},{3,2},{4,5},{5,4},{6,7},{7,6},{8,9},{9,8},{10,11... | collective-permute-start | bytes 1769480 | tf_op jit(solution)/shard_map/ppermute | solution.py:341
  421.0 9.1 %collective-permute-start.69 = (bf16[4,16,1792]{2,1,0:T(8,128)(2,1)S(1)}, bf16[4,16,1792]{2,1,0:T(8,128)(2,1)S(1)}, u32[]{:S(2)}, u32[]{:S(2)}) collective-permute-start(bf16[4,16,1792]{2,1,0:T(8,128)(2,1)S(1)} %select_select_fusion), channel_id=1, source_target_pairs={{0,4},{4,0},{8,12},{12,8},{16,20},{20,16},{24,28},{28,24},{1,5},{5... | collective-permute-start | bytes 688136 | tf_op jit(solution)/shard_map/ppermute | solution.py:341
  423.7 12.2 %collective-permute-start.58 = (bf16[2,4,16,1664]{3,2,1,0:T(8,128)(2,1)S(1)}, bf16[2,4,16,1664]{3,2,1,0:T(8,128)(2,1)S(1)}, u32[]{:S(2)}, u32[]{:S(2)}) collective-permute-start(bf16[2,4,16,1664]{3,2,1,0:T(8,128)(2,1)S(1)} %broadcast_select_fusion.4), channel_id=1, source_target_pairs={{0,4},{4,0},{8,12},{12,8},{16,20},{20,16},{24,28},{28,24},{1,5},{5... | collective-permute-start | bytes 1277960 | tf_op jit(solution)/shard_map/ppermute | solution.py:341
  430.2 8.5 %collective-permute-start.70 = (bf16[2,4,16,1792]{3,2,1,0:T(8,128)(2,1)S(1)}, bf16[2,4,16,1792]{3,2,1,0:T(8,128)(2,1)S(1)}, u32[]{:S(2)}, u32[]{:S(2)}) collective-permute-start(bf16[2,4,16,1792]{3,2,1,0:T(8,128)(2,1)S(1)} %broadcast_select_fusion.3), channel_id=1, source_target_pairs={{0,2},{1,3},{2,0},{3,1},{4,6},{5,7},{6,4},{7,5},{8,10},{9,11},{10,... | collective-permute-start | bytes 1376264 | tf_op jit(solution)/shard_map/ppermute | solution.py:341
  (83 other events, 547.2 us)
